TPU v7x, 128 devices: a whole 4x4x4 slice. The times are simulated.
128 devices in a mesh: row: 8 (over z, y_lo), col: 16 (over x, y_hi, core).
Axes of the slice: x: 4, y: 4 (y_hi: 2, y_lo: 2; y = y_hi * 2 + y_lo), z: 4, core: 2. Of those that a mesh axis runs over, the one named last changes fastest.
Arguments:
- pair_input: bfloat16 [384, 384, 128], P('row', 'col'), may hold values from -6 to 6
- chain_lengths: int32 [8], replicated, may hold values from 24 to 48, as said below
- input_gain: float32 [2, 128], replicated, may hold values from 0.1 to 1.9
- input_weight: bfloat16 [2, 128, 640], replicated, may hold values from -0.5 to 0.5
- output_gain: float32 [2, 128], replicated, may hold values from 0.1 to 1.9
- output_weight: bfloat16 [2, 128, 128], replicated, may hold values from -0.5 to 0.5
- cotangent: bfloat16 [384, 384, 128], P('row', 'col'), may hold values from -6 to 6
Outputs:
- pair_output: bfloat16 [384, 384, 128], P('row', 'col')
- pair_grad: float32 [384, 384, 128], P('row', 'col')
Inputs may be any that keep to these rules, and one draw needn't show every extreme that they name: `chain_lengths`: every chain has at least half of its 48 positions valid; in every draw at least one chain is entirely valid and one exactly half valid.
All inputs are finite; a program needn't handle non-finite values.
Results may differ from a plain program's by a relative error of at most 0.025.
Values may be sent and summed in bfloat16 or wider, within the bound.
A program may use at most 128 MiB of HBM per device.

v0:
```python
import jax
import jax.numpy as jnp
from jax import lax
from jax.sharding import PartitionSpec as P

CH = 128
N = 384
CHAINS = 8


EPSILON = 1e-05


def normalize(values):
    center = values - jnp.mean(values, axis=-1, keepdims=True)
    inverse = lax.rsqrt(jnp.mean(center * center, axis=-1, keepdims=True) + EPSILON)
    return (center * inverse, inverse)


def norm_backward(grad_normed, normed, inverse):
    return inverse * (
        grad_normed
        - jnp.mean(grad_normed, axis=-1, keepdims=True)
        - normed * jnp.mean(grad_normed * normed, axis=-1, keepdims=True)
    )


def token_valid(chain_lengths, offset, amount):
    positions = offset + jnp.arange(amount, dtype=jnp.int32)
    stride = N // CHAINS
    chain_index = positions // stride
    chosen = jnp.sum(
        jnp.where(
            chain_index[:, None] == jnp.arange(CHAINS, dtype=jnp.int32)[None, :],
            chain_lengths[None, :],
            0,
        ),
        axis=1,
    )
    return (positions % stride < chosen).astype(jnp.float32)


def project_pair(pair_state, norm_gain, weight, pair_mask):
    normed, inverse = normalize(pair_state.astype(jnp.float32))
    scaled = (normed * norm_gain).astype(jnp.bfloat16)
    mixed_all = jnp.dot(scaled, weight, preferred_element_type=jnp.float32)
    mask_cells = pair_mask[:, :, None]
    left_side = (
        jax.nn.sigmoid(mixed_all[..., CH : 2 * CH]) * mixed_all[..., :CH] * mask_cells
    ).astype(jnp.bfloat16)
    right_side = (
        jax.nn.sigmoid(mixed_all[..., 3 * CH : 4 * CH])
        * mixed_all[..., 2 * CH : 3 * CH]
        * mask_cells
    ).astype(jnp.bfloat16)
    return (mixed_all, left_side, right_side)


def finish_pair(pair_state, product, norm_gain, weight, mixed_all):
    normed, inverse = normalize(product)
    scaled = (normed * norm_gain).astype(jnp.bfloat16)
    projected = jnp.dot(scaled, weight, preferred_element_type=jnp.float32)
    return (
        pair_state.astype(jnp.float32) + jax.nn.sigmoid(mixed_all[..., 4 * CH :]) * projected
    ).astype(jnp.bfloat16)


def finish_back(upstream, product, norm_gain, weight, mixed_all):
    normed, inverse = normalize(product)
    scaled = (normed * norm_gain).astype(jnp.bfloat16)
    projected = jnp.dot(scaled, weight, preferred_element_type=jnp.float32)
    gate_value = jax.nn.sigmoid(mixed_all[..., 4 * CH :])
    grad_projected = (upstream * gate_value).astype(jnp.bfloat16)
    grad_gate = upstream * projected * gate_value * (1.0 - gate_value)
    grad_scaled = jnp.dot(grad_projected, weight.T, preferred_element_type=jnp.float32)
    grad_product = norm_backward(grad_scaled * norm_gain, normed, inverse)
    return (grad_product.astype(jnp.bfloat16), grad_gate)


def project_back(grad_left, grad_right, grad_gate, pair_state, norm_gain, weight, pair_mask):
    normed, inverse = normalize(pair_state.astype(jnp.float32))
    scaled = (normed * norm_gain).astype(jnp.bfloat16)
    mixed_all = jnp.dot(scaled, weight, preferred_element_type=jnp.float32)
    mask_cells = pair_mask[:, :, None]
    left_gate = jax.nn.sigmoid(mixed_all[..., CH : 2 * CH])
    right_gate = jax.nn.sigmoid(mixed_all[..., 3 * CH : 4 * CH])
    grad_mixed = jnp.concatenate(
        [
            grad_left * left_gate * mask_cells,
            grad_left * mixed_all[..., :CH] * mask_cells * left_gate * (1.0 - left_gate),
            grad_right * right_gate * mask_cells,
            grad_right
            * mixed_all[..., 2 * CH : 3 * CH]
            * mask_cells
            * right_gate
            * (1.0 - right_gate),
            grad_gate,
        ],
        axis=-1,
    ).astype(jnp.bfloat16)
    grad_scaled = jnp.dot(grad_mixed, weight.T, preferred_element_type=jnp.float32)
    return norm_backward(grad_scaled * norm_gain, normed, inverse)


def gather_columns(values):
    return lax.all_gather(values, "row", axis=0, tiled=True)


def gather_rows(values):
    return lax.all_gather(values, "col", axis=1, tiled=True)


def column_sums(term):
    return lax.psum_scatter(
        term.astype(jnp.bfloat16), "col", scatter_dimension=1, tiled=True
    ).astype(jnp.float32)


def row_sums(term):
    return lax.psum_scatter(
        term.astype(jnp.bfloat16), "row", scatter_dimension=0, tiled=True
    ).astype(jnp.float32)


def local(
    pair_input, chain_lengths, input_gain, input_weight, output_gain, output_weight, cotangent
):
    row_count = pair_input.shape[0]
    column_count = pair_input.shape[1]
    row_valid = token_valid(chain_lengths, lax.axis_index("row") * row_count, row_count)
    column_valid = token_valid(chain_lengths, lax.axis_index("col") * column_count, column_count)
    pair_mask = row_valid[:, None] * column_valid[None, :]
    mixed_out, left_out, right_out = project_pair(
        pair_input, input_gain[0], input_weight[0], pair_mask
    )
    kept_columns = None
    kept_columns = gather_columns(right_out)
    product_out = column_sums(
        jnp.einsum("ikc,jkc->ijc", left_out, kept_columns, preferred_element_type=jnp.float32)
    )
    pair_mid = finish_pair(pair_input, product_out, output_gain[0], output_weight[0], mixed_out)
    mixed_in, left_in, right_in = project_pair(pair_mid, input_gain[1], input_weight[1], pair_mask)
    left_in_rows = gather_rows(left_in)
    product_in = row_sums(
        jnp.einsum("kic,kjc->ijc", left_in_rows, right_in, preferred_element_type=jnp.float32)
    )
    pair_output = finish_pair(pair_mid, product_in, output_gain[1], output_weight[1], mixed_in)
    upstream = cotangent.astype(jnp.float32)
    grad_in, gate_in = finish_back(upstream, product_in, output_gain[1], output_weight[1], mixed_in)
    grad_in_columns = gather_columns(grad_in)
    grad_left_in = column_sums(
        jnp.einsum("ijc,kjc->kic", grad_in_columns, right_in, preferred_element_type=jnp.float32)
    )
    left_back = gather_rows(left_in)
    grad_right_in = jnp.einsum(
        "ijc,kic->kjc", grad_in_columns, left_back, preferred_element_type=jnp.float32
    )
    upstream_mid = upstream + project_back(
        grad_left_in, grad_right_in, gate_in, pair_mid, input_gain[1], input_weight[1], pair_mask
    )
    grad_out, gate_out = finish_back(
        upstream_mid, product_out, output_gain[0], output_weight[0], mixed_out
    )
    grad_out_rows = gather_rows(grad_out)
    right_back = gather_columns(right_out)
    grad_left_out = jnp.einsum(
        "ijc,jkc->ikc", grad_out_rows, right_back, preferred_element_type=jnp.float32
    )
    grad_right_out = row_sums(
        jnp.einsum("ijc,ikc->jkc", grad_out_rows, left_out, preferred_element_type=jnp.float32)
    )
    pair_grad = upstream_mid + project_back(
        grad_left_out,
        grad_right_out,
        gate_out,
        pair_input,
        input_gain[0],
        input_weight[0],
        pair_mask,
    )
    return (pair_output, pair_grad)


def solution(mesh):
    placed = (P("row", "col", None), P(), P(), P(), P(), P(), P("row", "col", None))
    return jax.shard_map(
        local,
        mesh=mesh,
        in_specs=placed,
        out_specs=(P("row", "col", None), P("row", "col", None)),
        check_vma=False,
    )
```

profile of v0, /device:TPU:1, one launch (start us, length us, event | category | flops | bytes accessed | tf_op | source)
XLA Modules:
  0.0 684.6 jit_solution(11213884457552859536)
XLA Ops:
  9.5 1.2 convert_reduce_fusion.1
  10.7 1.4 fusion.30
  12.2 1.8 fusion.106
  14.1 1.6 copy-done
  17.3 59.8 %all-gather.5.cloned.1.call-done = bf16[384,24,128]{2,1,0:T(8,128)(2,1)} async-done(((bf16[48,24,128]{2,1,0:T(8,128)(2,1)}), bf16[384,24,128]{2,1,0:T(8,128)(2,1)}) %all-gather.5.cloned.1.call-update) | async-done | bytes 2359312 | tf_op jit(solution)/shard_map/all_gather | solution.py:106
  77.0 3.7 copy.99
  80.7 3.6 convert_bitcast_fusion.1
  84.3 7.6 %copy.101 = bf16[48,384,128]{2,0,1:T(8,128)(2,1)} copy(bf16[48,384,128]{1,0,2:T(8,128)(2,1)} %convert_bitcast_fusion.1) | data formatting | bytes 9437184 | tf_op jit(solution)/shard_map/convert_element_type | solution.py:115
  92.6 80.5 %reduce-scatter.7.cloned.1.call-done = bf16[48,24,128]{2,0,1:T(8,128)(2,1)} async-done(((bf16[48,384,128]{2,0,1:T(8,128)(2,1)}), bf16[48,24,128]{2,0,1:T(8,128)(2,1)}) %reduce-scatter.7.cloned.1.call-update) | async-done | bytes 294928 | tf_op jit(solution)/shard_map/reduce_scatter | solution.py:114
  173.1 1.2 convert_reduce_fusion.3
  174.3 1.4 fusion.42
  175.7 2.6 convert_reduce_fusion
  179.9 1.7 copy-done.1
  183.0 2.4 copy.103
  185.4 59.5 %all-gather.7.cloned.1.call-done = bf16[48,384,128]{2,1,0:T(8,128)(2,1)} async-done(((bf16[48,24,128]{2,1,0:T(8,128)(2,1)}), bf16[48,384,128]{2,1,0:T(8,128)(2,1)}) %all-gather.7.cloned.1.call-update) | async-done | bytes 4718608 | tf_op jit(solution)/shard_map/all_gather | solution.py:110
  244.9 22.1 %copy.104 = bf16[48,384,128]{0,1,2:T(8,128)(2,1)} copy(bf16[48,384,128]{2,1,0:T(8,128)(2,1)} %all-gather.7.cloned.1.call-done) | data formatting | bytes 9437184 | tf_op jit(solution)/shard_map/all_gather | solution.py:110
  267.0 10.7 %convert_bitcast_fusion.3 = bf16[384,24,128]{0,1,2:T(8,128)(2,1)} fusion(bf16[48,24,128]{0,1,2:T(8,128)(2,1)} %copy.103, bf16[48,384,128]{0,1,2:T(8,128)(2,1)} %copy.104), kind=kOutput, calls=%fused_computation.4 | convolution fusion | flops 114425856 | bytes 7372800 | tf_op jit(solution)/shard_map/kic,kjc->ijc/dot_general | solution.py:145
  277.7 4.7 copy.105
  282.4 55.7 %reduce-scatter.9.cloned.1.call-done = bf16[48,24,128]{2,1,0:T(8,128)(2,1)} async-done(((bf16[384,24,128]{2,1,0:T(8,128)(2,1)}), bf16[48,24,128]{2,1,0:T(8,128)(2,1)}) %reduce-scatter.9.cloned.1.call-update) | async-done | bytes 294928 | tf_op jit(solution)/shard_map/reduce_scatter | solution.py:120
  339.3 1.4 fusion.36
  340.8 2.0 fusion.149
  342.8 1.4 fusion.35
  344.3 56.4 %all-gather.9.cloned.1.call-done = bf16[384,24,128]{2,1,0:T(8,128)(2,1)} async-done(((bf16[48,24,128]{2,1,0:T(8,128)(2,1)}), bf16[384,24,128]{2,1,0:T(8,128)(2,1)}) %all-gather.9.cloned.1.call-update) | async-done | bytes 2359312 | tf_op jit(solution)/shard_map/all_gather | solution.py:106
  400.8 4.8 copy.115
  405.6 5.4 convert_bitcast_fusion
  411.0 7.5 %copy.127 = bf16[48,384,128]{2,0,1:T(8,128)(2,1)} copy(bf16[48,384,128]{1,0,2:T(8,128)(2,1)} %convert_bitcast_fusion) | data formatting | bytes 9437184
  418.5 5.6 copy.149
  424.5 8.7 %fusion.151 = f32[128,48,24]{1,2,0:T(8,128)} fusion(bf16[48,384,128]{0,1,2:T(8,128)(2,1)} %copy.104, bf16[384,24,128]{0,1,2:T(8,128)(2,1)} %copy.115), kind=kOutput, calls=%fused_computation.218 | convolution fusion | flops 113246208 | bytes 7667712 | tf_op jit(solution)/shard_map/ijc,kic->kjc/dot_general | solution.py:155
  433.2 2.8 copy.119
  436.0 69.4 %reduce-scatter.13.cloned.1.call-done = bf16[24,6144]{1,0:T(8,128)(2,1)} async-done(((bf16[384,6144]{1,0:T(8,128)(2,1)}), bf16[24,6144]{1,0:T(8,128)(2,1)}) %reduce-scatter.13.cloned.1.call-update) | async-done | bytes 294928
  506.5 1.3 fusion.101
  507.9 1.6 fusion.100
  510.2 1.4 fusion.96
  512.6 3.1 fusion.147
  517.7 58.1 %all-gather.11.cloned.1.call-done = bf16[48,384,128]{2,0,1:T(8,128)(2,1)} async-done(((bf16[48,24,128]{2,0,1:T(8,128)(2,1)}), bf16[48,384,128]{2,0,1:T(8,128)(2,1)}) %all-gather.11.cloned.1.call-update) | async-done | bytes 4718608 | tf_op jit(solution)/shard_map/all_gather | solution.py:110
  575.8 17.8 %copy.122 = bf16[48,384,128]{0,1,2:T(8,128)(2,1)} copy(bf16[48,384,128]{2,0,1:T(8,128)(2,1)} %all-gather.11.cloned.1.call-done) | data formatting | bytes 9437184 | tf_op jit(solution)/shard_map/all_gather | solution.py:110
  593.6 10.4 %fusion.153 = bf16[128,24,384]{2,1,0:T(8,128)(2,1)} fusion(bf16[48,24,128]{0,1,2:T(8,128)(2,1)S(1)} %copy.100, bf16[48,384,128]{0,1,2:T(8,128)(2,1)} %copy.122), kind=kOutput, calls=%fused_computation.220 | convolution fusion | flops 113246208 | bytes 7372800 | tf_op jit(solution)/shard_map/ijc,ikc->jkc/dot_general | solution.py:170
  604.0 4.7 copy.126
  608.7 8.1 %fusion.152 = f32[128,24,48]{2,1,0:T(8,128)} fusion(bf16[384,24,128]{0,1,2:T(8,128)(2,1)S(1)} %copy.99, bf16[48,384,128]{0,1,2:T(8,128)(2,1)} %copy.122), kind=kOutput, calls=%fused_computation.219 | convolution fusion | flops 113246208 | bytes 7667712 | tf_op jit(solution)/shard_map/ijc,jkc->ikc/dot_general | solution.py:166
  616.7 1.9 copy.123
  618.6 2.0 fusion.95
  620.7 2.4 fusion.94
  623.1 41.5 %reduce-scatter.11.cloned.1.call-done = bf16[48,24,128]{2,1,0:T(8,128)(2,1)} async-done(((bf16[384,24,128]{2,1,0:T(8,128)(2,1)}), bf16[48,24,128]{2,1,0:T(8,128)(2,1)}) %reduce-scatter.11.cloned.1.call-update) | async-done | bytes 294928 | tf_op jit(solution)/shard_map/reduce_scatter | solution.py:120
  664.6 2.1 fusion.99
  666.7 2.4 fusion.98
  669.1 2.5 fusion.91
  671.6 2.1 fusion.146
  673.8 4.0 fusion.29
  (122 shorter events, 14.0 us)
Async XLA Ops:
  7.2 69.9 %all-gather.5.cloned.1.call-start = ((), (), s32[]{:S(2)}) async-start(), calls=%async_computation.4 | async-start | bytes 2654208 | tf_op jit(solution)/shard_map/all_gather | solution.py:106
  12.1 4.6 copy-start.20
  14.0 1.6 copy-start
  16.7 156.4 %reduce-scatter.7.cloned.1.call-start = ((), (), s32[]{:S(2)}) async-start(), calls=%async_computation.5 | async-start | bytes 5013504 | tf_op jit(solution)/shard_map/reduce_scatter | solution.py:114
  91.9 0.7 copy-start.34
  91.9 83.8 %copy-start.4 = (bf16[48,24,128]{2,1,0:T(8,128)(2,1)S(1)}, bf16[48,24,128]{2,1,0:T(8,128)(2,1)}, u32[]{:S(2)}) copy-start(bf16[48,24,128]{2,1,0:T(8,128)(2,1)} %param.7) | copy-start | bytes 884740
  91.9 153.0 %all-gather.7.cloned.1.call-start = ((), (), s32[]{:S(2)}) async-start(), calls=%async_computation.6 | async-start | bytes 5013504 | tf_op jit(solution)/shard_map/all_gather | solution.py:110
  174.3 4.0 copy-start.26
  175.7 3.3 copy-start.17
  175.7 2.6 copy-start.30
  178.3 0.7 copy-start.5
  179.9 1.7 copy-start.1
  182.7 155.4 %reduce-scatter.9.cloned.1.call-start = ((), (), s32[]{:S(2)}) async-start(), calls=%async_computation.7 | async-start | bytes 2654208 | tf_op jit(solution)/shard_map/reduce_scatter | solution.py:120
  282.4 118.4 %all-gather.9.cloned.1.call-start = ((), (), s32[]{:S(2)}) async-start(), calls=%async_computation.8 | async-start | bytes 2654208 | tf_op jit(solution)/shard_map/all_gather | solution.py:106
  339.3 3.5 copy-start.9
  339.3 3.4 copy-start.28
  340.8 2.0 copy-start.32
  344.3 161.1 %reduce-scatter.13.cloned.1.call-start = ((), (), s32[]{:S(2)}) async-start(), calls=%async_computation.11 | async-start | bytes 5013504
  424.2 151.6 %all-gather.11.cloned.1.call-start = ((), (), s32[]{:S(2)}) async-start(), calls=%async_computation.9 | async-start | bytes 5013504 | tf_op jit(solution)/shard_map/all_gather | solution.py:110
  505.4 4.2 copy-start.2
  505.4 4.2 copy-start.3
  507.8 2.3 copy-start.10
  507.8 2.3 copy-start.13
  507.8 2.3 copy-start.29
  507.8 2.3 copy-start.33
  507.9 2.3 copy-start.35
  510.2 1.4 copy-start.6
  510.2 1.4 copy-start.18
  511.6 1.0 copy-start.8
  511.6 1.0 copy-start.27
  511.6 1.0 copy-start.31
  512.4 3.3 copy-start.11
  512.5 3.2 copy-start.22
  512.5 3.2 copy-start.24
  517.4 147.3 %reduce-scatter.11.cloned.1.call-start = ((), (), s32[]{:S(2)}) async-start(), calls=%async_computation.10 | async-start | bytes 2654208 | tf_op jit(solution)/shard_map/reduce_scatter | solution.py:120
  620.7 48.4 %copy-start.7 = (bf16[48,24,128]{2,1,0:T(8,128)(2,1)S(1)}, bf16[48,24,128]{2,1,0:T(8,128)(2,1)}, u32[]{:S(2)}) copy-start(bf16[48,24,128]{2,1,0:T(8,128)(2,1)} %copy-done.5) | copy-start | bytes 884740
  620.7 48.4 %copy-start.12 = (f32[48,24,128]{2,1,0:T(8,128)S(1)}, f32[48,24,128]{2,1,0:T(8,128)}, u32[]{:S(2)}) copy-start(f32[48,24,128]{2,1,0:T(8,128)} %copy-done.11) | copy-start | bytes 1769476
  620.7 48.4 %copy-start.14 = (bf16[48,24,128]{2,1,0:T(8,128)(2,1)S(1)}, bf16[48,24,128]{2,1,0:T(8,128)(2,1)}, u32[]{:S(2)}) copy-start(bf16[48,24,128]{2,1,0:T(8,128)(2,1)} %param.13) | copy-start | bytes 884740
  620.7 48.4 %copy-start.15 = (f32[48,24,128]{2,1,0:T(8,128)S(1)}, f32[48,24,128]{2,1,0:T(8,128)}, u32[]{:S(2)}) copy-start(f32[48,24,128]{2,1,0:T(8,128)} %get-tuple-element.22) | copy-start | bytes 1769476
  620.7 48.4 %copy-start.23 = (f32[48,24]{1,0:T(8,128)S(1)}, f32[48,24]{1,0:T(8,128)}, u32[]{:S(2)}) copy-start(f32[48,24]{1,0:T(8,128)} %copy-done.22) | copy-start | bytes 13828
  620.7 48.4 %copy-start.25 = (f32[48,24]{1,0:T(8,128)S(1)}, f32[48,24]{1,0:T(8,128)}, u32[]{:S(2)}) copy-start(f32[48,24]{1,0:T(8,128)} %copy-done.24) | copy-start | bytes 13828
  666.7 4.9 copy-start.19
  666.7 4.9 copy-start.21
  669.1 4.7 copy-start.16
Sparse Core Ops, SparseCore 0:
  16.8 60.1 all-gather.4
  92.0 81.0 reduce-scatter.6
  182.9 61.9 all-gather.6
  282.5 55.5 reduce-scatter.8
  344.4 56.3 all-gather.8
  424.3 80.9 reduce-scatter.12
  517.5 58.2 all-gather.10
  608.8 55.7 reduce-scatter.10
where the time goes:
time: 686 us; the launch traced here: 685 us
  waiting for transfers between devices  481 us (70%)
  local copies, waits for them, and re-layouts  93.1 us (14%)
  matrix products  61.5 us (9%)
  other arithmetic  33.2 us (5%)
  between operations  14.8 us (2%)
    all_gather x2, waiting for transfers between devices, gather_rows(): return lax.all_gather(values, 'col', axis=1, tiled=True)  118 us
    all_gather x2, waiting for transfers between devices, gather_columns(): return lax.all_gather(values, 'row', axis=0, tiled=True)  116 us
    reduce_scatter x2, waiting for transfers between devices, row_sums(): lax.psum_scatter(term.astype(jnp.bfloat16), 'row', scatter_dimension=0, t...  97.2 us
    reduce_scatter x1, waiting for transfers between devices, column_sums(): lax.psum_scatter(term.astype(jnp.bfloat16), 'col', scatter_dimension=1, t...  80.5 us
    unnamed x9, waiting for transfers between devices  69.5 us
    all_gather x2, local copies, waits for them, and re-layouts, gather_rows(): return lax.all_gather(values, 'col', axis=1, tiled=True)  39.9 us
    unnamed x75, local copies, waits for them, and re-layouts  18.7 us
  transfers between devices with their start and end apart: 8, of which 8 were waited for; matrix products, arithmetic and copies ran while one was open for 4% of the time, Pallas kernels for 0%

commit v1 on v0

--- a/solution.py
+++ b/solution.py
@@ -102,24 +102,32 @@
     return norm_backward(grad_scaled * norm_gain, normed, inverse)
 
 
-def gather_columns(values):
-    return lax.all_gather(values, "row", axis=0, tiled=True)
+AXES = ("row", "col")
 
 
-def gather_rows(values):
-    return lax.all_gather(values, "col", axis=1, tiled=True)
+def to_channels(*parts):
+    rows, columns, channels = parts[0].shape
+    packed = jnp.stack([p.reshape(rows * columns, channels).T for p in parts], axis=1)
+    moved = lax.all_to_all(packed, AXES, split_axis=0, concat_axis=0, tiled=True)
+    grid = moved.reshape(lax.axis_size("row"), lax.axis_size("col"), len(parts), rows, columns)
+    grid = grid.transpose(2, 0, 3, 1, 4)
+    return [grid[i].reshape(N, N) for i in range(len(parts))]
 
 
-def column_sums(term):
-    return lax.psum_scatter(
-        term.astype(jnp.bfloat16), "col", scatter_dimension=1, tiled=True
-    ).astype(jnp.float32)
+def to_blocks(*parts):
+    across, down = lax.axis_size("row"), lax.axis_size("col")
+    rows, columns = N // across, N // down
+    packed = jnp.stack(parts).astype(jnp.bfloat16)
+    packed = packed.reshape(len(parts), across, rows, down, columns).transpose(1, 3, 0, 2, 4)
+    packed = packed.reshape(across * down, len(parts), rows * columns)
+    moved = lax.all_to_all(packed, AXES, split_axis=0, concat_axis=0, tiled=True)
+    return [
+        moved[:, i].T.reshape(rows, columns, -1).astype(jnp.float32) for i in range(len(parts))
+    ]
 
 
-def row_sums(term):
-    return lax.psum_scatter(
-        term.astype(jnp.bfloat16), "row", scatter_dimension=0, tiled=True
-    ).astype(jnp.float32)
+def multiply(form, first, second):
+    return jnp.einsum(form, first, second, preferred_element_type=jnp.float32)
 
 
 def local(
@@ -133,27 +141,18 @@
     mixed_out, left_out, right_out = project_pair(
         pair_input, input_gain[0], input_weight[0], pair_mask
     )
-    kept_columns = None
-    kept_columns = gather_columns(right_out)
-    product_out = column_sums(
-        jnp.einsum("ikc,jkc->ijc", left_out, kept_columns, preferred_element_type=jnp.float32)
-    )
+    left_0, right_0 = to_channels(left_out, right_out)
+    (product_out,) = to_blocks(multiply("ik,jk->ij", left_0, right_0))
     pair_mid = finish_pair(pair_input, product_out, output_gain[0], output_weight[0], mixed_out)
     mixed_in, left_in, right_in = project_pair(pair_mid, input_gain[1], input_weight[1], pair_mask)
-    left_in_rows = gather_rows(left_in)
-    product_in = row_sums(
-        jnp.einsum("kic,kjc->ijc", left_in_rows, right_in, preferred_element_type=jnp.float32)
-    )
+    left_1, right_1 = to_channels(left_in, right_in)
+    (product_in,) = to_blocks(multiply("ki,kj->ij", left_1, right_1))
     pair_output = finish_pair(pair_mid, product_in, output_gain[1], output_weight[1], mixed_in)
     upstream = cotangent.astype(jnp.float32)
     grad_in, gate_in = finish_back(upstream, product_in, output_gain[1], output_weight[1], mixed_in)
-    grad_in_columns = gather_columns(grad_in)
-    grad_left_in = column_sums(
-        jnp.einsum("ijc,kjc->kic", grad_in_columns, right_in, preferred_element_type=jnp.float32)
-    )
-    left_back = gather_rows(left_in)
-    grad_right_in = jnp.einsum(
-        "ijc,kic->kjc", grad_in_columns, left_back, preferred_element_type=jnp.float32
+    (grad_1,) = to_channels(grad_in)
+    grad_left_in, grad_right_in = to_blocks(
+        multiply("ij,kj->ki", grad_1, right_1), multiply("ij,ki->kj", grad_1, left_1)
     )
     upstream_mid = upstream + project_back(
         grad_left_in, grad_right_in, gate_in, pair_mid, input_gain[1], input_weight[1], pair_mask
@@ -161,13 +160,9 @@
     grad_out, gate_out = finish_back(
         upstream_mid, product_out, output_gain[0], output_weight[0], mixed_out
     )
-    grad_out_rows = gather_rows(grad_out)
-    right_back = gather_columns(right_out)
-    grad_left_out = jnp.einsum(
-        "ijc,jkc->ikc", grad_out_rows, right_back, preferred_element_type=jnp.float32
-    )
-    grad_right_out = row_sums(
-        jnp.einsum("ijc,ikc->jkc", grad_out_rows, left_out, preferred_element_type=jnp.float32)
+    (grad_0,) = to_channels(grad_out)
+    grad_left_out, grad_right_out = to_blocks(
+        multiply("ij,jk->ik", grad_0, right_0), multiply("ij,ik->jk", grad_0, left_0)
     )
     pair_grad = upstream_mid + project_back(
         grad_left_out,

time: 686 us -> 378 us (0.55)
  waiting for transfers between devices: 481 us -> 26.5 us
  blocking collectives: 0 us -> 95.9 us
  local copies, waits for them, and re-layouts: 93.1 us -> 158 us
  matrix products: 61.5 us -> 18.4 us
  other arithmetic: 33.2 us -> 53.7 us
  starting transfers between devices: 0.99 us -> 17.7 us
  between operations: 14.8 us -> 1.88 us
    all_gather x4 -> x0, waiting for transfers between devices: 234 us -> none  [the longest x2 118 us: gather_rows(): return lax.all_gather(values, 'col', axis=1, tiled=True)]
    reduce_scatter x3 -> x0, waiting for transfers between devices: 178 us -> none  [the longest x2 97.2 us: row_sums(): lax.psum_scatter(term.astype(jnp.bfloat16), 'row', scatter_dimension=0, t...]
    all_to_all x0 -> x5, blocking collectives: none -> 95.9 us  [the longest x3 60.4 us: to_channels(): lax.all_to_all(packed, AXES, split_axis=0, concat_axis=0, tiled=True)]
    unnamed x9 -> x0, waiting for transfers between devices: 69.5 us -> none
    reshape x0 -> x19, local copies, waits for them, and re-layouts: none -> 59.8 us  [the longest x7 30.2 us: to_blocks(): packed = packed.reshape(across * down, len(parts), rows * columns)]
    all_gather x4 -> x0, local copies, waits for them, and re-layouts: 48.5 us -> none  [the longest x2 39.9 us: gather_rows(): return lax.all_gather(values, 'col', axis=1, tiled=True)]
    dot_general x6, matrix products: 46.9 us -> 7.5 us  [multiply(): return jnp.einsum(form, first, second, preferred_element_type=jnp.float32)]
    all_to_all x0 -> x3, waiting for transfers between devices: none -> 26.5 us  [the longest x2 20 us: to_blocks(): lax.all_to_all(packed, AXES, split_axis=0, concat_axis=0, tiled=True)]
  transfers between devices with their start and end apart: 8 -> 3, of which waited for: 8 -> 3; matrix products, arithmetic and copies ran while one was open for 4% -> 3% of each run, Pallas kernels for 0% -> 0%
where the time goes in v1:
time: 378 us; the launch traced here: 372 us
  local copies, waits for them, and re-layouts  158 us (42%)
  blocking collectives  95.9 us (25%)
  other arithmetic  53.7 us (14%)
  waiting for transfers between devices  26.5 us (7%)
  matrix products  18.4 us (5%)
  starting transfers between devices  17.7 us (5%)
    all_to_all x3, blocking collectives, to_channels(): lax.all_to_all(packed, AXES, split_axis=0, concat_axis=0, tiled=True)  60.4 us
    all_to_all x2, blocking collectives, to_blocks(): lax.all_to_all(packed, AXES, split_axis=0, concat_axis=0, tiled=True)  35.4 us
    reshape x7, local copies, waits for them, and re-layouts, to_blocks(): packed = packed.reshape(across * down, len(parts), rows * columns)  30.2 us
    slice x8, local copies, waits for them, and re-layouts, to_channels(): return [grid[i].reshape(N, N) for i in range(len(parts))]  23.5 us
    unnamed x124, local copies, waits for them, and re-layouts  23 us
    all_to_all x2, waiting for transfers between devices, to_blocks(): lax.all_to_all(packed, AXES, split_axis=0, concat_axis=0, tiled=True)  20 us
    reshape x4, local copies, waits for them, and re-layouts, to_channels(): moved.reshape(lax.axis_size('row'), lax.axis_size('col'), len(parts), row...  19.7 us
    another operation x6, local copies, waits for them, and re-layouts, to_channels(): return [grid[i].reshape(N, N) for i in range(len(parts))]  14 us
  transfers between devices with their start and end apart: 3, of which 3 were waited for; matrix products, arithmetic and copies ran while one was open for 3% of the time, Pallas kernels for 0%

profile of v1, /device:TPU:1, one launch (start us, length us, event | category | flops | bytes accessed | tf_op | source)
XLA Modules:
  0.0 372.4 jit_solution(5553755197691416920)
XLA Ops:
  11.1 25.7 %all_to_all.40 = bf16[128,2,1152]{2,1,0:T(2,128)(2,1)S(1)} all-to-all(bf16[128,2,1152]{2,1,0:T(2,128)(2,1)S(1)} %copy.160), channel_id=1, replica_groups=mesh['row'=8,'col'=16] {'row','col'}, dimensions={0} | all-to-all | bytes 1179648 | tf_op jit(solution)/shard_map/all_to_all | solution.py:111
  36.9 5.5 %reshape.340 = bf16[8,16,2,48,24]{4,3,1,0,2:T(8,128)(2,1)} reshape(bf16[128,2,1152]{2,0,1:T(8,128)(2,1)S(1)} %copy.161) | data formatting | bytes 1179648 | tf_op jit(solution)/shard_map/reshape | solution.py:112
  42.4 4.2 %fusion.101 = (bf16[1,8,48,16,24]{4,2,3,1,0:T(8,128)(2,1)}, bf16[1,8,48,16,24]{4,2,3,1,0:T(8,128)(2,1)}) fusion(bf16[2,8,48,16,24]{4,2,3,1,0:T(8,128)(2,1)} %bitcast.239), kind=kLoop, calls=%fused_computation.189 | loop fusion | bytes 1179648 | tf_op jit(solution)/shard_map/slice | solution.py:114
  46.6 2.5 copy.163
  50.9 2.6 copy.162
  59.0 2.7 copy.165
  61.7 4.0 %reshape.382 = bf16[128,1,1152]{2,1,0:T(2,128)(2,1)S(1)} reshape(bf16[8,16,1,48,24]{4,3,1,0,2:T(8,128)(2,1)} %copy.165) | data formatting | bytes 589824 | tf_op jit(solution)/shard_map/reshape | solution.py:122
  66.3 3.1 reduce.12
  71.5 6.1 %all-to-all-start.1 = ((bf16[128,2,576]{2,1,0:T(2,128)(2,1)}), bf16[128,2,576]{2,1,0:T(2,128)(2,1)}, u32[]{:S(2)}, u32[]{:S(2)}) async-start(bf16[128,2,576]{2,1,0:T(2,128)(2,1)} %reshape.389), calls=%async_computation.1 | async-start | bytes 655360 | tf_op jit(solution)/shard_map/all_to_all | solution.py:123
  78.1 10.8 %all-to-all-done.1 = bf16[128,2,576]{2,1,0:T(2,128)(2,1)} async-done(((bf16[128,2,576]{2,1,0:T(2,128)(2,1)}), bf16[128,2,576]{2,1,0:T(2,128)(2,1)}, u32[]{:S(2)}, u32[]{:S(2)}) %all-to-all-start.1) | async-done | bytes 294944 | tf_op jit(solution)/shard_map/all_to_all | solution.py:123
  89.0 3.2 reshape.390
  105.6 18.0 %all_to_all.41 = bf16[128,2,1152]{2,1,0:T(2,128)(2,1)S(1)} all-to-all(bf16[128,2,1152]{2,1,0:T(2,128)(2,1)S(1)} %copy.170), channel_id=1, replica_groups=mesh['row'=8,'col'=16] {'row','col'}, dimensions={0} | all-to-all | bytes 1179648 | tf_op jit(solution)/shard_map/all_to_all | solution.py:111
  124.6 6.2 %reshape.345 = bf16[8,16,2,48,24]{4,3,1,0,2:T(8,128)(2,1)} reshape(bf16[128,2,1152]{2,0,1:T(8,128)(2,1)} %copy.171) | data formatting | bytes 1179648 | tf_op jit(solution)/shard_map/reshape | solution.py:112
  130.8 4.2 %fusion.100 = (bf16[1,8,48,16,24]{4,2,3,1,0:T(8,128)(2,1)}, bf16[1,8,48,16,24]{4,2,3,1,0:T(8,128)(2,1)}) fusion(bf16[2,8,48,16,24]{4,2,3,1,0:T(8,128)(2,1)} %bitcast.240), kind=kLoop, calls=%fused_computation.188 | loop fusion | bytes 1179648 | tf_op jit(solution)/shard_map/slice | solution.py:114
  135.0 2.5 copy.173
  139.9 2.5 copy.172
  147.2 2.5 reshape.346
  149.7 2.6 copy.175
  152.4 4.7 %reshape.383 = bf16[128,1,1152]{2,1,0:T(2,128)(2,1)} reshape(bf16[8,16,1,48,24]{4,3,1,0,2:T(8,128)(2,1)} %copy.175) | data formatting | bytes 589824 | tf_op jit(solution)/shard_map/reshape | solution.py:122
  157.0 3.4 reduce.13
  161.4 17.1 %all_to_all.42 = bf16[128,2,576]{2,1,0:T(2,128)(2,1)} all-to-all(bf16[128,2,576]{2,1,0:T(2,128)(2,1)} %reshape.391), channel_id=1, replica_groups=mesh['row'=8,'col'=16] {'row','col'}, dimensions={0} | all-to-all | bytes 589824 | tf_op jit(solution)/shard_map/all_to_all | solution.py:123
  178.5 3.2 reshape.392
  194.2 2.5 reduce.14
  198.7 5.9 %all-to-all-start.4 = ((bf16[128,2,576]{2,1,0:T(2,128)(2,1)}), bf16[128,2,576]{2,1,0:T(2,128)(2,1)}, u32[]{:S(2)}, u32[]{:S(2)}) async-start(bf16[128,2,576]{2,1,0:T(2,128)(2,1)} %reshape.393), calls=%async_computation.4 | async-start | bytes 655360 | tf_op jit(solution)/shard_map/all_to_all | solution.py:111
  204.6 2.5 copy.178
  209.5 6.5 %all-to-all-done.4 = bf16[128,2,576]{2,1,0:T(2,128)(2,1)} async-done(((bf16[128,2,576]{2,1,0:T(2,128)(2,1)}), bf16[128,2,576]{2,1,0:T(2,128)(2,1)}, u32[]{:S(2)}, u32[]{:S(2)}) %all-to-all-start.4) | async-done | bytes 294944 | tf_op jit(solution)/shard_map/all_to_all | solution.py:111
  216.0 3.2 reshape.394
  219.2 3.4 reduce.10
  222.6 4.0 %reshape.350 = bf16[8,16,1,48,24]{4,3,1,0,2:T(8,128)(2,1)} reshape(bf16[128,1152]{1,0:T(8,128)(2,1)} %reduce.10) | data formatting | bytes 589824 | tf_op jit(solution)/shard_map/reshape | solution.py:112
  226.6 2.5 copy.184
  229.1 3.0 copy.181
  234.6 3.5 reshape.375
  242.1 4.5 %copy.207 = bf16[8,16,2,48,24]{4,3,2,1,0:T(8,128)(2,1)} copy(bf16[8,16,2,48,24]{3,4,1,0,2:T(8,128)(2,1)} %maximum_bitcast_fusion) | data formatting | bytes 1179648 | tf_op jit(solution)/shard_map/reshape | solution.py:122
  246.5 6.3 %reshape.385 = bf16[128,2,1152]{2,1,0:T(2,128)(2,1)} reshape(bf16[8,16,2,48,24]{4,3,2,1,0:T(8,128)(2,1)} %copy.207) | data formatting | bytes 1179648 | tf_op jit(solution)/shard_map/reshape | solution.py:122
  252.9 5.7 %all-to-all-start.5 = ((bf16[128,2,1152]{2,1,0:T(2,128)(2,1)}), bf16[128,2,1152]{2,1,0:T(2,128)(2,1)}, u32[]{:S(2)}, u32[]{:S(2)}) async-start(bf16[128,2,1152]{2,1,0:T(2,128)(2,1)} %reshape.385), calls=%async_computation.5 | async-start | bytes 1179648 | tf_op jit(solution)/shard_map/all_to_all | solution.py:123
  263.3 9.2 %all-to-all-done.5 = bf16[128,2,1152]{2,1,0:T(2,128)(2,1)} async-done(((bf16[128,2,1152]{2,1,0:T(2,128)(2,1)}), bf16[128,2,1152]{2,1,0:T(2,128)(2,1)}, u32[]{:S(2)}, u32[]{:S(2)}) %all-to-all-start.5) | async-done | bytes 589856 | tf_op jit(solution)/shard_map/all_to_all | solution.py:123
  272.5 3.3 slice_convert_fusion.2
  291.2 16.7 %all_to_all.43 = bf16[128,2,576]{2,1,0:T(2,128)(2,1)} all-to-all(bf16[128,2,576]{2,1,0:T(2,128)(2,1)S(1)} %reshape.395), channel_id=1, replica_groups=mesh['row'=8,'col'=16] {'row','col'}, dimensions={0} | all-to-all | bytes 589824 | tf_op jit(solution)/shard_map/all_to_all | solution.py:111
  307.9 2.5 reshape.396
  310.4 2.5 reduce.11
  312.9 4.0 %reshape.354 = bf16[8,16,1,48,24]{4,3,1,0,2:T(8,128)(2,1)} reshape(bf16[128,1152]{1,0:T(8,128)(2,1)} %reduce.11) | data formatting | bytes 589824 | tf_op jit(solution)/shard_map/reshape | solution.py:112
  316.9 2.5 copy.194
  319.4 2.5 copy.192
  321.9 2.5 reshape_squeeze.23
  328.3 4.5 %copy.210 = bf16[8,16,2,48,24]{4,3,2,1,0:T(8,128)(2,1)} copy(bf16[8,16,2,48,24]{3,4,1,0,2:T(8,128)(2,1)} %maximum_bitcast_fusion.1) | data formatting | bytes 1179648 | tf_op jit(solution)/shard_map/reshape | solution.py:122
  332.8 5.7 %reshape.386 = bf16[128,2,1152]{2,1,0:T(2,128)(2,1)S(1)} reshape(bf16[8,16,2,48,24]{4,3,2,1,0:T(8,128)(2,1)} %copy.210) | data formatting | bytes 1179648 | tf_op jit(solution)/shard_map/reshape | solution.py:122
  338.4 18.3 %all_to_all.44 = bf16[128,2,1152]{2,1,0:T(2,128)(2,1)S(1)} all-to-all(bf16[128,2,1152]{2,1,0:T(2,128)(2,1)S(1)} %reshape.386), channel_id=1, replica_groups=mesh['row'=8,'col'=16] {'row','col'}, dimensions={0} | all-to-all | bytes 1179648 | tf_op jit(solution)/shard_map/all_to_all | solution.py:123
  368.1 3.9 %fusion.23 = (f32[48,24,128]{2,1,0:T(8,128)}, bf16[48,24,128]{2,1,0:T(8,128)(2,1)}) fusion(bf16[48,24,128]{2,1,0:T(8,128)(2,1)S(1)} %copy-done.5, f32[48,24,128]{2,1,0:T(8,128)S(1)} %get-tuple-element.36, f32[48,24]{1,0:T(8,128)S(1)} %broadcast_multiply_fusion.1, f32[48,24]{1,0:T(8,128)S(1)} %broadcast_multiply_fusion.2, f32[48,24]{1,0:T(8,128)S(1)} %copy-done.44, ...), kind=kLoop, calls=%fused_computation.44 | loop fusion | flops 3391488 | bytes 4165632 | tf_op jit(solution)/shard_map/add | solution.py:167
  (218 shorter events, 101.6 us)
Async XLA Ops:
  2.9 2.7 copy-start.50
  2.9 94.1 %copy-start.52 = (f32[128]{0:T(128)}, f32[128]{0:T(128)S(1)}, u32[]{:S(2)}) copy-start(f32[128]{0:T(128)S(1)} %get-tuple-element.28) | copy-start | bytes 1540
  4.2 1.5 copy-start.32
  5.6 2.4 copy-start.10
  50.9 5.0 %copy-start.14 = (bf16[384,384]{0,1:T(8,128)(2,1)}, bf16[384,384]{0,1:T(8,128)(2,1)S(1)}, u32[]{:S(2)}) copy-start(bf16[384,384]{0,1:T(8,128)(2,1)S(1)} %reshape_squeeze.19) | copy-start | bytes 884740
  65.7 11.9 %copy-start.56 = (f32[2,128]{1,0:T(2,128)S(1)}, f32[2,128]{1,0:T(2,128)}, u32[]{:S(2)}) copy-start(f32[2,128]{1,0:T(2,128)} %param.11) | copy-start | bytes 3076
  71.5 17.5 %all-to-all-start.1 = ((bf16[128,2,576]{2,1,0:T(2,128)(2,1)}), bf16[128,2,576]{2,1,0:T(2,128)(2,1)}, u32[]{:S(2)}, u32[]{:S(2)}) async-start(bf16[128,2,576]{2,1,0:T(2,128)(2,1)} %reshape.389), calls=%async_computation.1 | async-start | bytes 655360 | tf_op jit(solution)/shard_map/all_to_all | solution.py:123
  77.6 17.1 %copy-start.4 = (bf16[48,24,128]{2,1,0:T(8,128)(2,1)S(1)}, bf16[48,24,128]{2,1,0:T(8,128)(2,1)}, u32[]{:S(2)}) copy-start(bf16[48,24,128]{2,1,0:T(8,128)(2,1)} %param.7) | copy-start | bytes 884740
  78.1 18.5 %copy-start.54 = (f32[128]{0:T(128)}, f32[128]{0:T(128)S(1)}, u32[]{:S(2)}) copy-start(f32[128]{0:T(128)S(1)} %get-tuple-element.27) | copy-start | bytes 1540
  94.3 2.4 copy-start.49
  94.7 3.0 copy-start.34
  97.7 2.4 copy-start.11
  98.5 1.6 copy-start
  188.6 2.2 copy-start.17
  188.6 2.2 copy-start.47
  188.6 2.2 copy-start.48
  198.7 17.3 %all-to-all-start.4 = ((bf16[128,2,576]{2,1,0:T(2,128)(2,1)}), bf16[128,2,576]{2,1,0:T(2,128)(2,1)}, u32[]{:S(2)}, u32[]{:S(2)}) async-start(bf16[128,2,576]{2,1,0:T(2,128)(2,1)} %reshape.393), calls=%async_computation.4 | async-start | bytes 655360 | tf_op jit(solution)/shard_map/all_to_all | solution.py:111
  238.0 1.9 copy-start.9
  238.0 1.9 copy-start.22
  252.9 19.6 %all-to-all-start.5 = ((bf16[128,2,1152]{2,1,0:T(2,128)(2,1)}), bf16[128,2,1152]{2,1,0:T(2,128)(2,1)}, u32[]{:S(2)}, u32[]{:S(2)}) async-start(bf16[128,2,1152]{2,1,0:T(2,128)(2,1)} %reshape.385), calls=%async_computation.5 | async-start | bytes 1179648 | tf_op jit(solution)/shard_map/all_to_all | solution.py:123
  279.3 1.6 copy-start.2
  279.3 3.2 copy-start.1
  279.3 3.2 copy-start.12
  283.6 1.3 copy-start.7
  283.6 1.3 copy-start.25
  283.6 1.3 copy-start.30
  283.6 1.3 copy-start.35
  283.6 1.3 copy-start.53
  285.7 1.6 copy-start.18
  285.7 1.6 copy-start.41
  285.7 1.6 copy-start.43
  319.4 5.0 %copy-start.15 = (bf16[384,384]{0,1:T(8,128)(2,1)S(1)}, bf16[384,384]{0,1:T(8,128)(2,1)}, u32[]{:S(2)}) copy-start(bf16[384,384]{0,1:T(8,128)(2,1)} %copy-done.14) | copy-start | bytes 884740
  321.9 4.2 %copy-start.23 = (bf16[384,384]{0,1:T(8,128)(2,1)S(1)}, bf16[384,384]{0,1:T(8,128)(2,1)}, u32[]{:S(2)}) copy-start(bf16[384,384]{0,1:T(8,128)(2,1)} %reshape_squeeze.18) | copy-start | bytes 884740
  324.4 1.8 copy-start.38
  362.1 1.4 copy-start.3
  362.1 2.4 copy-start.13
  364.6 1.1 copy-start.19
  364.6 1.2 copy-start.21
  364.6 1.2 copy-start.26
  364.6 1.4 copy-start.27
  364.6 1.4 copy-start.31
  364.6 1.4 copy-start.42
  364.6 1.4 copy-start.44
  365.2 1.8 copy-start.5
  365.3 1.8 copy-start.33
  365.3 1.8 copy-start.36
  365.3 1.8 copy-start.40
  365.3 1.8 copy-start.51
  (13 other events, 12.0 us)

commit v2 on v1

v2 whole, which is shorter than its diff:
```python
import functools

import jax
import jax.numpy as jnp
from jax import lax
from jax.experimental import pallas as pl
from jax.experimental.pallas import tpu as pltpu
from jax.sharding import PartitionSpec as P

MESH = pl.DeviceIdType.MESH
F32 = jnp.float32
BF16 = jnp.bfloat16

CH = 128
N = 384
CHAINS = 8
EPSILON = 1e-05

ROWS, COLS = 8, 16
DEVICES = ROWS * COLS
HEIGHT, WIDTH = N // ROWS, N // COLS
HALF = 64
TILES = WIDTH // 2
LANES = TILES * 128
STEP = 256
STEPS = LANES // STEP
SIDE = CHAINS * HALF


def column_pair(tile):
    return (tile, tile + 8) if tile < 8 else (tile + 8, tile + 12)


def sigmoid(values):
    return 0.5 * jnp.tanh(0.5 * values) + 0.5


def mean_rows(values):
    return jnp.sum(values, axis=0, keepdims=True) * (1.0 / values.shape[0])


def normalize(values):
    center = values - mean_rows(values)
    inverse = lax.rsqrt(mean_rows(center * center) + EPSILON)
    return center * inverse, inverse


def norm_backward(grad_normed, normed, inverse):
    return inverse * (
        grad_normed - mean_rows(grad_normed) - normed * mean_rows(grad_normed * normed)
    )


def dot(first, second, first_dim=1, second_dim=0):
    return lax.dot_general(
        first, second, (((first_dim,), (second_dim,)), ((), ())), preferred_element_type=F32
    )


def swap_halves(values):
    return pltpu.roll(values, HALF, axis=len(values.shape) - 1)


def lower_lanes(shape):
    return lax.broadcasted_iota(jnp.int32, shape, len(shape) - 1) % 128 < HALF


def merge(first, second):
    lower = lower_lanes(first.shape)
    return (
        jnp.where(lower, first, swap_halves(second)),
        jnp.where(lower, swap_halves(first), second),
    )


def kernel(
    x_ref,
    length_ref,
    ig_ref,
    iw_ref,
    og_ref,
    ow_ref,
    ct_ref,
    out_ref,
    grad_ref,
    flat,
    state,
    upstream,
    mixed,
    norm_in,
    inverse_in,
    norm_out,
    inverse_out,
    projected,
    swap,
    gains,
    weight_t,
    out_weight_t,
    left,
    right,
    grad,
    result,
    send_wide,
    send_slim,
    wide_0,
    wide_1,
    wide_2,
    wide_3,
    slim_0,
    slim_1,
    slim_2,
    slim_3,
    send_sem,
    recv_sem,
):
    row, col = lax.axis_index("row"), lax.axis_index("col")
    me = row * COLS + col

    barrier = pltpu.get_barrier_semaphore()

    def greet(t, carry):
        peer = (lax.rem(row + t // COLS, ROWS), lax.rem(col + t % COLS, COLS))
        pl.semaphore_signal(barrier, inc=1, device_id=peer, device_id_type=MESH)
        return carry

    lax.fori_loop(1, DEVICES, greet, 0)

    def send(phase, source, target):
        def one(t, carry):
            offset = lax.rem(t * 9, DEVICES)
            peer = (lax.rem(row + offset // COLS, ROWS), lax.rem(col + offset % COLS, COLS))
            pltpu.make_async_remote_copy(
                source.at[peer[0] * COLS + peer[1]],
                target.at[me],
                send_sem.at[phase],
                recv_sem.at[phase],
                device_id=peer,
                device_id_type=MESH,
            ).start()
            return carry

        lax.fori_loop(1, DEVICES, one, 0)
        target[me] = source[me]

    def receive(phase, source, target):
        others = pl.ds(0, DEVICES - 1)
        copies = pltpu.make_async_remote_copy(
            source.at[others],
            target.at[others],
            send_sem.at[phase],
            recv_sem.at[phase],
            device_id=(row, col),
            device_id_type=MESH,
        )
        copies.wait_send()
        copies.wait_recv()

    def steps(body):
        def one(s, carry):
            body(pl.ds(pl.multiple_of(s * STEP, STEP), STEP))
            return carry

        lax.fori_loop(0, STEPS, one, 0)

    def valid(at):
        lane = lax.broadcasted_iota(jnp.int32, (1, STEP), 1) + at.start
        tile = lane // 128
        token = lane % HALF
        upper = (lane // HALF) % 2
        column = tile + jnp.where(tile < 8, 8 * upper, 8 + 4 * upper) + (col % 2) * WIDTH
        inside = (token < length_ref[row]) & (column < length_ref[col // 2])
        return jnp.where(inside, 1.0, 0.0)

    def load_block(source, target):
        flat[...] = source[...].astype(F32)
        empty = jnp.zeros((HALF - HEIGHT, CH), F32)
        for tile in range(TILES):
            parts = []
            for column in column_pair(tile):
                parts += [flat[pl.ds(column, HEIGHT, stride=WIDTH), :], empty]
            target[:, tile * 128 : (tile + 1) * 128] = jnp.concatenate(parts, axis=0).T

    def store_block(source, target):
        for tile in range(TILES):
            block = source[:, tile * 128 : (tile + 1) * 128].T
            for half, column in enumerate(column_pair(tile)):
                target[pl.ds(column, HEIGHT, stride=WIDTH), :] = block[
                    half * HALF : half * HALF + HEIGHT
                ]

    def project(u):
        def body(at):
            normed, inverse = normalize(state[:, at])
            norm_in[u, :, at] = normed
            inverse_in[u, :, at] = inverse
            scaled = (normed * gains[u]).astype(BF16)
            mixed[u, :, at] = dot(weight_t[u], scaled)

        steps(body)

    def pack_wide(first, second):
        for tile in range(TILES):
            at = pl.ds(tile * 128, 128)
            lower, upper = merge(first(at), second(at))
            one, two = column_pair(tile)
            swap[pl.ds(one, CH, stride=WIDTH), :] = lower
            swap[pl.ds(two, CH, stride=WIDTH), :] = upper

        def one(c, carry):
            at = pl.ds(pl.multiple_of(c * 16 * WIDTH, 16 * WIDTH), 16 * WIDTH)
            send_wide[pl.ds(c * 16, 16)] = swap[at, :].astype(BF16).reshape(16, WIDTH, 128)
            return carry

        lax.fori_loop(0, CH // 16, one, 0)

    def unpack(source, rows):
        def one(c, carry):
            at = pl.ds(pl.multiple_of(c * 16 * rows, 16 * rows), 16 * rows)
            swap[at, :] = source[pl.ds(c * 16, 16)].astype(F32).reshape(16 * rows, 128)
            return carry

        lax.fori_loop(0, CH // 16, one, 0)

    def pack_slim(first):
        for tile in range(TILES):
            swap[pl.ds(tile, CH, stride=16), :] = first[:, tile * 128 : (tile + 1) * 128]

        def one(c, carry):
            at = pl.ds(pl.multiple_of(c * 256, 256), 256)
            send_slim[pl.ds(c * 16, 16)] = swap[at, :].astype(BF16).reshape(16, 16, 128)
            return carry

        lax.fori_loop(0, CH // 16, one, 0)

    def edges(u):
        def body(at):
            keep = valid(at)
            norm_out[u, :, at] = (
                sigmoid(mixed[u, CH : 2 * CH, at]) * mixed[u, 0:CH, at] * keep
            )
            projected[u, :, at] = (
                sigmoid(mixed[u, 3 * CH : 4 * CH, at]) * mixed[u, 2 * CH : 3 * CH, at] * keep
            )

        steps(body)
        pack_wide(lambda at: norm_out[u, :, at], lambda at: projected[u, :, at])

    def blocks(body):
        def one(s, carry):
            chain = s // 4
            pair = s % 4
            body(
                chain,
                pair,
                pl.ds(pl.multiple_of(chain * HALF, HALF), HALF),
                pl.ds(pl.multiple_of(pair * 128, 128), 128),
            )
            return carry

        lax.fori_loop(0, CHAINS * 4, one, 0)

    def assemble_wide(source, first, second):
        def body(chain, pair, down, across):
            firsts, seconds = [], []
            for part in range(2):
                at = pair * 2 * COLS + chain * 2 + part
                one, two = merge(source[at].astype(F32), source[at + COLS].astype(F32))
                firsts.append(one)
                seconds.append(two)
            empty = jnp.zeros((HALF - 2 * WIDTH, 128), F32)
            first[down, across] = jnp.concatenate(firsts + [empty], axis=0).astype(BF16)
            second[down, across] = jnp.concatenate(seconds + [empty], axis=0).astype(BF16)

        blocks(body)

    def assemble_slim(source, target):
        def body(chain, pair, down, across):
            parts = []
            for part in range(2):
                at = pair * 2 * COLS + chain * 2 + part
                one, two = merge(source[at].astype(F32), source[at + COLS].astype(F32))
                low = lax.broadcasted_iota(jnp.int32, (8, 128), 0) < 4
                last = jnp.where(low, one[8:16], pltpu.roll(two[8:16], 4, axis=0))
                parts += [one[0:8], two[0:8], last]
            empty = jnp.zeros((HALF - 2 * WIDTH, 128), F32)
            target[down, across] = jnp.concatenate(parts + [empty], axis=0).astype(BF16)

        blocks(body)

    def split_wide(first, second):
        def body(chain, pair, down, across):
            lower, upper = merge(first[down, across], second[down, across])
            for part in range(2):
                at = pair * 2 * COLS + chain * 2 + part
                cut = slice(part * WIDTH, (part + 1) * WIDTH)
                send_wide[at] = lower[cut].astype(BF16)
                send_wide[at + COLS] = upper[cut].astype(BF16)

        blocks(body)

    def split_slim(source):
        def body(chain, pair, down, across):
            values = source[down, across]
            for part in range(2):
                at = pair * 2 * COLS + chain * 2 + part
                cut = values[part * WIDTH : (part + 1) * WIDTH]
                last = cut[16:24]
                low_0, low_1 = merge(cut[0:8], cut[8:16])
                high_0, high_1 = merge(last, pltpu.roll(last, 4, axis=0))
                send_slim[at] = jnp.concatenate([low_0, high_0], axis=0).astype(BF16)
                send_slim[at + COLS] = jnp.concatenate([low_1, high_1], axis=0).astype(BF16)

        blocks(body)

    def finish(u, source):
        unpack(source, 16)
        for tile in range(TILES):
            norm_out[u, :, tile * 128 : (tile + 1) * 128] = swap[pl.ds(tile, CH, stride=16), :]

        def body(at):
            normed, inverse = normalize(norm_out[u, :, at])
            norm_out[u, :, at] = normed
            inverse_out[u, :, at] = inverse
            scaled = (normed * gains[2 + u]).astype(BF16)
            values = dot(out_weight_t[u], scaled)
            projected[u, :, at] = values
            gate = sigmoid(mixed[u, 4 * CH :, at])
            state[:, at] = (state[:, at] + gate * values).astype(BF16).astype(F32)

        steps(body)

    def finish_back(u):
        def body(at):
            up = upstream[:, at]
            gate = sigmoid(mixed[u, 4 * CH :, at])
            grad_projected = up * gate
            mixed[u, 4 * CH :, at] = grad_projected * projected[u, :, at] * (1.0 - gate)
            grad_scaled = dot(ow_ref[u], grad_projected.astype(BF16))
            projected[u, :, at] = norm_backward(
                grad_scaled * gains[2 + u], norm_out[u, :, at], inverse_out[u, :, at]
            )

        steps(body)
        pack_slim(projected.at[u])

    def project_back(u, source):
        unpack(source, WIDTH)
        for tile in range(TILES):
            at = slice(tile * 128, (tile + 1) * 128)
            one, two = column_pair(tile)
            lower, upper = merge(
                swap[pl.ds(one, CH, stride=WIDTH), :], swap[pl.ds(two, CH, stride=WIDTH), :]
            )
            norm_out[u, :, at] = lower
            projected[u, :, at] = upper

        def body(at):
            keep = valid(at)
            parts = []
            for values, base in ((norm_out, 0), (projected, 2 * CH)):
                gate = sigmoid(mixed[u, base + CH : base + 2 * CH, at])
                direct = values[u, :, at] * gate * keep
                parts.append(direct.astype(BF16))
                parts.append((direct * mixed[u, base : base + CH, at] * (1.0 - gate)).astype(BF16))
            parts.append(mixed[u, 4 * CH :, at].astype(BF16))
            grad_scaled = dot(iw_ref[u], jnp.concatenate(parts, axis=0))
            upstream[:, at] = upstream[:, at] + norm_backward(
                grad_scaled * gains[u], norm_in[u, :, at], inverse_in[u, :, at]
            )

        steps(body)

    for u in range(2):
        weight_t[u] = iw_ref[u].astype(F32).T.astype(BF16)
        out_weight_t[u] = ow_ref[u].astype(F32).T.astype(BF16)
        for i, ref in ((u, ig_ref), (2 + u, og_ref)):
            spread = jnp.broadcast_to(ref[u : u + 1, :], (CH, CH)).T
            gains[i] = jnp.concatenate([spread, spread], axis=1)

    load_block(x_ref, state)
    project(0)
    edges(0)
    pl.semaphore_wait(barrier, DEVICES - 1)
    send(0, send_wide, wide_0)
    load_block(ct_ref, upstream)
    receive(0, send_wide, wide_0)
    assemble_wide(wide_0, left.at[0], right.at[0])
    result[0] = dot(right[0], left[0], 0, 0)
    split_slim(result.at[0])
    send(1, send_slim, slim_0)
    receive(1, send_slim, slim_0)

    finish(0, slim_0)
    project(1)
    edges(1)
    send(2, send_wide, wide_1)
    receive(2, send_wide, wide_1)
    assemble_wide(wide_1, left.at[1], right.at[1])
    result[0] = dot(right[1], left[1], 1, 1)
    split_slim(result.at[0])
    send(3, send_slim, slim_1)
    receive(3, send_slim, slim_1)

    finish(1, slim_1)
    finish_back(1)
    send(4, send_slim, slim_2)
    store_block(state, flat)
    out_ref[...] = flat[...].astype(BF16)
    receive(4, send_slim, slim_2)
    assemble_slim(slim_2, grad)
    result[0] = dot(grad[...], right[1], 0, 0)
    result[1] = dot(grad[...], left[1], 1, 0)
    split_wide(result.at[0], result.at[1])
    send(5, send_wide, wide_2)
    receive(5, send_wide, wide_2)

    project_back(1, wide_2)
    finish_back(0)
    send(6, send_slim, slim_3)
    receive(6, send_slim, slim_3)
    assemble_slim(slim_3, grad)
    result[0] = dot(right[0], grad[...], 1, 0)
    result[1] = dot(left[0], grad[...], 1, 1)
    split_wide(result.at[0], result.at[1])
    send(7, send_wide, wide_3)
    receive(7, send_wide, wide_3)

    project_back(0, wide_3)
    store_block(upstream, grad_ref)


def local(
    pair_input, chain_lengths, input_gain, input_weight, output_gain, output_weight, cotangent
):
    cells = HEIGHT * WIDTH
    vmem = pl.BlockSpec(memory_space=pltpu.VMEM)
    smem = pl.BlockSpec(memory_space=pltpu.SMEM)
    wide = pltpu.VMEM((DEVICES, WIDTH, 128), BF16)
    slim = pltpu.VMEM((DEVICES, 16, 128), BF16)
    plane = pltpu.VMEM((CH, LANES), F32)
    planes = pltpu.VMEM((2, CH, LANES), F32)
    line = pltpu.VMEM((2, 1, LANES), F32)
    out, grad = pl.pallas_call(
        kernel,
        out_shape=(
            jax.ShapeDtypeStruct((cells, CH), BF16),
            jax.ShapeDtypeStruct((cells, CH), F32),
        ),
        in_specs=[vmem, smem, vmem, vmem, vmem, vmem, vmem],
        out_specs=(vmem, vmem),
        scratch_shapes=[
            pltpu.VMEM((cells, CH), F32),
            plane,
            plane,
            pltpu.VMEM((2, 5 * CH, LANES), F32),
            planes,
            line,
            planes,
            line,
            planes,
            pltpu.VMEM((CH * WIDTH, 128), F32),
            pltpu.VMEM((4, CH, STEP), F32),
            pltpu.VMEM((2, 5 * CH, CH), BF16),
            pltpu.VMEM((2, CH, CH), BF16),
            pltpu.VMEM((2, SIDE, SIDE), BF16),
            pltpu.VMEM((2, SIDE, SIDE), BF16),
            pltpu.VMEM((SIDE, SIDE), BF16),
            pltpu.VMEM((2, SIDE, SIDE), F32),
            wide,
            slim,
            wide,
            wide,
            wide,
            wide,
            slim,
            slim,
            slim,
            slim,
            pltpu.SemaphoreType.DMA((8,)),
            pltpu.SemaphoreType.DMA((8,)),
        ],
        compiler_params=pltpu.CompilerParams(
            collective_id=0, has_side_effects=True, vmem_limit_bytes=52 * 2**20
        ),
    )(
        pair_input.reshape(cells, CH),
        chain_lengths,
        input_gain,
        input_weight,
        output_gain,
        output_weight,
        cotangent.reshape(cells, CH),
    )
    shape = (HEIGHT, WIDTH, CH)
    return out.reshape(shape), grad.reshape(shape)


def solution(mesh):
    placed = (P("row", "col", None), P(), P(), P(), P(), P(), P("row", "col", None))
    return jax.shard_map(
        local,
        mesh=mesh,
        in_specs=placed,
        out_specs=(P("row", "col", None), P("row", "col", None)),
        check_vma=False,
    )
```

time: 378 us -> 148 us (0.39); the launches traced: 372 us -> 148 us
  local copies, waits for them, and re-layouts: 158 us -> 5.94 us
  Pallas kernels: 0 us -> 141 us
  blocking collectives: 95.9 us -> 0 us
  other arithmetic: 53.7 us -> 0 us
  waiting for transfers between devices: 26.5 us -> 0 us
  matrix products: 18.4 us -> 0 us
  starting transfers between devices: 17.7 us -> 0 us
    pallas_call x0 -> x1, Pallas kernels: none -> 141 us  [local(): pl.pallas_call(kernel, out_shape=(jax.ShapeDtypeStruct((cells, CH), BF16)...]
    all_to_all x5 -> x0, blocking collectives: 95.9 us -> none  [the longest x3 60.4 us: to_channels(): lax.all_to_all(packed, AXES, split_axis=0, concat_axis=0, tiled=True)]
    reshape x19 -> x0, local copies, waits for them, and re-layouts: 59.8 us -> none  [the longest x7 30.2 us: to_blocks(): packed = packed.reshape(across * down, len(parts), rows * columns)]
    all_to_all x3 -> x0, waiting for transfers between devices: 26.5 us -> none  [the longest x2 20 us: to_blocks(): lax.all_to_all(packed, AXES, split_axis=0, concat_axis=0, tiled=True)]
    slice x8 -> x0, local copies, waits for them, and re-layouts: 23.5 us -> none  [to_channels(): return [grid[i].reshape(N, N) for i in range(len(parts))]]
    dot_general x14 -> x0, matrix products: 18.4 us -> none  [the longest x6 7.5 us: multiply(): return jnp.einsum(form, first, second, preferred_element_type=jnp.float32)]
    all_to_all x3 -> x0, starting transfers between devices: 17.7 us -> none  [the longest x2 11.8 us: to_blocks(): lax.all_to_all(packed, AXES, split_axis=0, concat_axis=0, tiled=True)]
    unnamed x124 -> x16, local copies, waits for them, and re-layouts: 23 us -> 5.94 us
  transfers between devices with their start and end apart: 3 -> 0, of which waited for: 3 -> 0; matrix products, arithmetic and copies ran while one was open for 3% -> 0% of each run, Pallas kernels for 0% -> 0%
where the time goes in v2:
time: 148 us
  Pallas kernels  141 us (95%)
  local copies, waits for them, and re-layouts  5.94 us (4%)
    pallas_call x1, Pallas kernels, local(): pl.pallas_call(kernel, out_shape=(jax.ShapeDtypeStruct((cells, CH), BF16)...  141 us
    unnamed x16, local copies, waits for them, and re-layouts  5.94 us

profile of v2, /device:TPU:1, one launch (start us, length us, event | category | flops | bytes accessed | tf_op | source)
XLA Modules:
  0.0 147.9 jit_solution(5971991011242447342)
XLA Ops:
  0.6 0.0 copy-start.5
  0.6 0.0 copy-start.4
  0.7 0.0 copy-start.6
  0.7 0.7 copy-done.5
  1.3 0.0 copy-done.4
  1.3 0.0 copy-done.6
  1.3 0.0 copy-start
  1.3 1.0 copy-done
  2.3 0.0 copy-start.1
  2.3 1.0 copy-done.1
  3.3 0.0 copy-start.2
  3.3 1.0 copy-done.2
  4.2 0.0 copy-start.3
  4.2 0.8 copy-done.3
  5.1 141.3 %shard_map.86 = (bf16[1152,128]{1,0:T(8,128)(2,1)S(1)}, f32[1152,128]{1,0:T(8,128)S(1)}) custom-call(bf16[1152,128]{1,0:T(8,128)(2,1)S(1)} %bitcast.5, s32[8]{0:T(128)S(1)} %copy-done.6, f32[2,128]{1,0:T(2,128)S(1)} %copy-done.4, bf16[2,128,640]{2,1,0:T(8,128)(2,1)S(1)} %copy-done, f32[2,128]{1,0:T(2,128)S(1)} %copy-done.5, ...), custom_call_target="tpu_custom_call" | custom-call | tf_op jit(solution)/shard_map/pallas_call | solution.py:443
  146.3 0.7 copy.11
  147.1 0.8 copy.12
Async XLA Ops:
  0.6 0.7 copy-start.5
  0.6 0.7 copy-start.4
  0.7 0.7 copy-start.6
  1.3 1.0 copy-start
  2.3 1.0 copy-start.1
  3.3 1.0 copy-start.2
  4.2 0.8 copy-start.3

commit v3 on v2

v3 whole, which is shorter than its diff:
```python
import functools

import jax
import jax.numpy as jnp
from jax import lax
from jax.experimental import pallas as pl
from jax.experimental.pallas import tpu as pltpu
from jax.sharding import PartitionSpec as P

MESH = pl.DeviceIdType.MESH
F32 = jnp.float32
BF16 = jnp.bfloat16

CH = 128
N = 384
CHAINS = 8
EPSILON = 1e-05

ROWS, COLS = 8, 16
DEVICES = ROWS * COLS
HEIGHT, WIDTH = N // ROWS, N // COLS
HALF = 64
TILES = WIDTH // 2
LANES = TILES * 128
STEP = 256
STEPS = LANES // STEP
SIDE = CHAINS * HALF


def column_pair(tile):
    return (tile, tile + 8) if tile < 8 else (tile + 8, tile + 12)


def sigmoid(values):
    return 0.5 * jnp.tanh(0.5 * values) + 0.5


def mean_rows(values):
    return jnp.sum(values, axis=0, keepdims=True) * (1.0 / values.shape[0])


def normalize(values):
    center = values - mean_rows(values)
    inverse = lax.rsqrt(mean_rows(center * center) + EPSILON)
    return center * inverse, inverse


def norm_backward(grad_normed, normed, inverse):
    return inverse * (
        grad_normed - mean_rows(grad_normed) - normed * mean_rows(grad_normed * normed)
    )


def dot(first, second, first_dim=1, second_dim=0):
    return lax.dot_general(
        first, second, (((first_dim,), (second_dim,)), ((), ())), preferred_element_type=F32
    )


def swap_halves(values):
    return pltpu.roll(values, HALF, axis=len(values.shape) - 1)


def lower_lanes(shape):
    return lax.broadcasted_iota(jnp.int32, shape, len(shape) - 1) % 128 < HALF


def merge(first, second):
    lower = lower_lanes(first.shape)
    return (
        jnp.where(lower, first, swap_halves(second)),
        jnp.where(lower, swap_halves(first), second),
    )


def kernel(
    x_hbm,
    length_ref,
    ig_ref,
    iw_hbm,
    og_ref,
    ow_hbm,
    ct_hbm,
    out_hbm,
    grad_hbm,
    block,
    iw_ref,
    ow_ref,
    ct_ref,
    flat,
    state,
    upstream,
    mixed,
    norm_in,
    inverse_in,
    norm_out,
    inverse_out,
    projected,
    swap,
    inbox,
    gains,
    weight_t,
    out_weight_t,
    left,
    right,
    grad,
    result,
    send_wide,
    send_slim,
    wide_0,
    wide_1,
    wide_2,
    wide_3,
    slim_0,
    slim_1,
    slim_2,
    slim_3,
    send_sem,
    recv_sem,
    copy_sem,
):
    row, col = lax.axis_index("row"), lax.axis_index("col")
    me = row * COLS + col
    my_chain = col // 2

    loads = [
        pltpu.make_async_copy(source, target, copy_sem.at[i])
        for i, (source, target) in enumerate(
            ((x_hbm, block), (iw_hbm, iw_ref), (ow_hbm, ow_ref), (ct_hbm, ct_ref))
        )
    ]
    for copy in loads:
        copy.start()

    barrier = pltpu.get_barrier_semaphore()

    def greet(t, carry):
        peer = (lax.rem(row + t // COLS, ROWS), lax.rem(col + t % COLS, COLS))
        pl.semaphore_signal(barrier, inc=1, device_id=peer, device_id_type=MESH)
        return carry

    lax.fori_loop(1, DEVICES, greet, 0)

    def send(phase, source, target, chain):
        for step in range(ROWS):
            for part in range(2):
                peer = (lax.rem(row + step, ROWS), chain * 2 + part)
                at = peer[0] * COLS + peer[1]

                def start():
                    pltpu.make_async_remote_copy(
                        source.at[at],
                        target.at[me],
                        send_sem.at[phase],
                        recv_sem.at[phase, my_chain],
                        device_id=peer,
                        device_id_type=MESH,
                    ).start()

                if step > 0:
                    start()
                else:

                    @pl.when(at != me)
                    def _():
                        start()

                    @pl.when(at == me)
                    def _():
                        target[me] = source[me]

    def send_all(body):
        def one(s, carry):
            body(lax.rem(my_chain + s, CHAINS))
            return carry

        lax.fori_loop(0, CHAINS, one, 0)

    def receive(phase, source, target, body):
        def arrived(count):
            some = pl.ds(0, count)
            return pltpu.make_async_remote_copy(
                source.at[some],
                target.at[some],
                send_sem.at[phase],
                recv_sem.at[phase, my_chain],
                device_id=(row, col),
                device_id_type=MESH,
            )

        def one(s, carry):
            chain = lax.rem(my_chain + CHAINS - s, CHAINS)

            def wait(count):
                some = pl.ds(0, count)
                pltpu.make_async_remote_copy(
                    source.at[some],
                    target.at[some],
                    send_sem.at[phase],
                    recv_sem.at[phase, chain],
                    device_id=(row, col),
                    device_id_type=MESH,
                ).wait_recv()

            @pl.when(s == 0)
            def _():
                wait(2 * ROWS - 1)

            @pl.when(s > 0)
            def _():
                wait(2 * ROWS)

            body(chain)
            return carry

        lax.fori_loop(0, CHAINS, one, 0)
        arrived(DEVICES - 1).wait_send()

    def steps(body):
        def one(s, carry):
            body(s, pl.ds(pl.multiple_of(s * STEP, STEP), STEP))
            return carry

        lax.fori_loop(0, STEPS, one, 0)

    def tiles_of(s):
        pairs = []
        for i in range(2):
            tile = s * 2 + i
            late = tile >= 8
            pairs.append((tile + jnp.where(late, 8, 0), tile + jnp.where(late, 12, 8)))
        return pairs

    def valid(s):
        lane = lax.broadcasted_iota(jnp.int32, (1, STEP), 1) + s * STEP
        tile = lane // 128
        token = lane % HALF
        upper = (lane // HALF) % 2
        column = tile + jnp.where(tile < 8, 8 * upper, 8 + 4 * upper) + (col % 2) * WIDTH
        inside = (token < length_ref[row]) & (column < length_ref[my_chain])
        return jnp.where(inside, 1.0, 0.0)

    def load_block(source, target):
        flat[...] = source[...].astype(F32)
        empty = jnp.zeros((HALF - HEIGHT, CH), F32)
        for tile in range(TILES):
            parts = []
            for column in column_pair(tile):
                parts += [flat[pl.ds(column, HEIGHT, stride=WIDTH), :], empty]
            target[:, tile * 128 : (tile + 1) * 128] = jnp.concatenate(parts, axis=0).T

    def store_block(source, target):
        for tile in range(TILES):
            values = source[:, tile * 128 : (tile + 1) * 128].T
            for half, column in enumerate(column_pair(tile)):
                target[pl.ds(column, HEIGHT, stride=WIDTH), :] = values[
                    half * HALF : half * HALF + HEIGHT
                ]

    def put_wide(s, first, second):
        for i, (one, two) in enumerate(tiles_of(s)):
            at = slice(i * 128, (i + 1) * 128)
            lower, upper = merge(first[:, at], second[:, at])
            swap[pl.ds(one, CH, stride=WIDTH), :] = lower
            swap[pl.ds(two, CH, stride=WIDTH), :] = upper

    def get_wide(s):
        firsts, seconds = [], []
        for one, two in tiles_of(s):
            lower, upper = merge(
                inbox[pl.ds(one, CH, stride=WIDTH), :], inbox[pl.ds(two, CH, stride=WIDTH), :]
            )
            firsts.append(lower)
            seconds.append(upper)
        return jnp.concatenate(firsts, axis=1), jnp.concatenate(seconds, axis=1)

    def put_slim(s, values):
        for i in range(2):
            swap[pl.ds(s * 2 + i, CH, stride=16), :] = values[:, i * 128 : (i + 1) * 128]

    def get_slim(s):
        return jnp.concatenate(
            [inbox[pl.ds(s * 2 + i, CH, stride=16), :] for i in range(2)], axis=1
        )

    def channels_of(chain, rows):
        for device_row in range(ROWS):
            at = device_row * COLS + chain * 2
            yield pl.ds(at, 2), pl.ds(pl.multiple_of(at * rows, 2 * rows), 2 * rows)

    def send_swap(phase, source, target, rows):
        def body(chain):
            for messages, at in channels_of(chain, rows):
                source[messages] = swap[at, :].astype(BF16).reshape(2, rows, 128)
            send(phase, source, target, chain)

        send_all(body)

    def receive_swap(phase, source, target, rows):
        def body(chain):
            for messages, at in channels_of(chain, rows):
                inbox[at, :] = target[messages].astype(F32).reshape(2 * rows, 128)

        receive(phase, source, target, body)

    def project(u, s, at, values):
        normed, inverse = normalize(values)
        norm_in[u, :, at] = normed
        inverse_in[u, :, at] = inverse
        mix = dot(weight_t[u], (normed * gains[u]).astype(BF16))
        mixed[u, :, at] = mix
        keep = valid(s)
        put_wide(
            s,
            sigmoid(mix[CH : 2 * CH]) * mix[0:CH] * keep,
            sigmoid(mix[3 * CH : 4 * CH]) * mix[2 * CH : 3 * CH] * keep,
        )

    def finish(u, s, at):
        normed, inverse = normalize(get_slim(s))
        norm_out[u, :, at] = normed
        inverse_out[u, :, at] = inverse
        values = dot(out_weight_t[u], (normed * gains[2 + u]).astype(BF16))
        projected[u, :, at] = values
        gate = sigmoid(mixed[u, 4 * CH :, at])
        after = (state[:, at] + gate * values).astype(BF16).astype(F32)
        state[:, at] = after
        return after, normed, inverse, values, gate

    def finish_back(u, s, at, up, normed, inverse, values, gate):
        grad_projected = up * gate
        mixed[u, 4 * CH :, at] = grad_projected * values * (1.0 - gate)
        grad_scaled = dot(ow_ref[u], grad_projected.astype(BF16))
        put_slim(s, norm_backward(grad_scaled * gains[2 + u], normed, inverse))

    def project_back(u, s, at):
        keep = valid(s)
        parts = []
        for values, base in zip(get_wide(s), (0, 2 * CH)):
            gate = sigmoid(mixed[u, base + CH : base + 2 * CH, at])
            direct = values * gate * keep
            parts.append(direct.astype(BF16))
            parts.append((direct * mixed[u, base : base + CH, at] * (1.0 - gate)).astype(BF16))
        parts.append(mixed[u, 4 * CH :, at].astype(BF16))
        grad_scaled = dot(iw_ref[u], jnp.concatenate(parts, axis=0))
        after = upstream[:, at] + norm_backward(
            grad_scaled * gains[u], norm_in[u, :, at], inverse_in[u, :, at]
        )
        upstream[:, at] = after
        return after

    def places(chain):
        down = pl.ds(pl.multiple_of(chain * HALF, HALF), HALF)
        for pair in range(ROWS // 2):
            indices = [pair * 2 * COLS + chain * 2 + part for part in range(2)]
            yield down, slice(pair * 128, (pair + 1) * 128), indices

    empty = jnp.zeros((HALF - 2 * WIDTH, 128), F32)

    def assemble_wide(phase, source, first, second):
        def body(chain):
            for down, across, indices in places(chain):
                firsts, seconds = [], []
                for at in indices:
                    one, two = merge(source[at].astype(F32), source[at + COLS].astype(F32))
                    firsts.append(one)
                    seconds.append(two)
                first[down, across] = jnp.concatenate(firsts + [empty], axis=0).astype(BF16)
                second[down, across] = jnp.concatenate(seconds + [empty], axis=0).astype(BF16)

        receive(phase, send_wide, source, body)

    def assemble_slim(phase, source, target):
        def body(chain):
            low = lax.broadcasted_iota(jnp.int32, (8, 128), 0) < 4
            for down, across, indices in places(chain):
                parts = []
                for at in indices:
                    one, two = merge(source[at].astype(F32), source[at + COLS].astype(F32))
                    last = jnp.where(low, one[8:16], pltpu.roll(two[8:16], 4, axis=0))
                    parts += [one[0:8], two[0:8], last]
                target[down, across] = jnp.concatenate(parts + [empty], axis=0).astype(BF16)

        receive(phase, send_slim, source, body)

    def split_wide(phase, first, second, target):
        def body(chain):
            for down, across, indices in places(chain):
                lower, upper = merge(first[down, across], second[down, across])
                for part, at in enumerate(indices):
                    cut = slice(part * WIDTH, (part + 1) * WIDTH)
                    send_wide[at] = lower[cut].astype(BF16)
                    send_wide[at + COLS] = upper[cut].astype(BF16)
            send(phase, send_wide, target, chain)

        send_all(body)

    def split_slim(phase, source, target):
        def body(chain):
            for down, across, indices in places(chain):
                values = source[down, across]
                for part, at in enumerate(indices):
                    cut = values[part * WIDTH : (part + 1) * WIDTH]
                    last = cut[16:24]
                    low_0, low_1 = merge(cut[0:8], cut[8:16])
                    high_0, high_1 = merge(last, pltpu.roll(last, 4, axis=0))
                    send_slim[at] = jnp.concatenate([low_0, high_0], axis=0).astype(BF16)
                    send_slim[at + COLS] = jnp.concatenate([low_1, high_1], axis=0).astype(BF16)
            send(phase, send_slim, target, chain)

        send_all(body)

    loads[0].wait()
    load_block(block, state)
    loads[1].wait()
    loads[2].wait()
    for u in range(2):
        weight_t[u] = iw_ref[u].astype(F32).T.astype(BF16)
        out_weight_t[u] = ow_ref[u].astype(F32).T.astype(BF16)
        for i, ref in ((u, ig_ref), (2 + u, og_ref)):
            spread = jnp.broadcast_to(ref[u : u + 1, :], (CH, CH)).T
            gains[i] = jnp.concatenate([spread, spread], axis=1)

    steps(lambda s, at: project(0, s, at, state[:, at]))
    pl.semaphore_wait(barrier, DEVICES - 1)
    send_swap(0, send_wide, wide_0, WIDTH)
    loads[3].wait()
    load_block(ct_ref, upstream)
    assemble_wide(0, wide_0, left.at[0], right.at[0])
    result[0] = dot(right[0], left[0], 0, 0)
    split_slim(1, result.at[0], slim_0)
    receive_swap(1, send_slim, slim_0, 16)

    def middle(s, at):
        project(1, s, at, finish(0, s, at)[0])

    steps(middle)
    send_swap(2, send_wide, wide_1, WIDTH)
    assemble_wide(2, wide_1, left.at[1], right.at[1])
    result[0] = dot(right[1], left[1], 1, 1)
    split_slim(3, result.at[0], slim_1)
    receive_swap(3, send_slim, slim_1, 16)

    def top(s, at):
        _, normed, inverse, values, gate = finish(1, s, at)
        finish_back(1, s, at, upstream[:, at], normed, inverse, values, gate)

    steps(top)
    send_swap(4, send_slim, slim_2, 16)
    store_block(state, flat)
    block[...] = flat[...].astype(BF16)
    store = pltpu.make_async_copy(block, out_hbm, copy_sem.at[0])
    store.start()
    assemble_slim(4, slim_2, grad)
    result[0] = dot(grad[...], right[1], 0, 0)
    result[1] = dot(grad[...], left[1], 1, 0)
    split_wide(5, result.at[0], result.at[1], wide_2)
    receive_swap(5, send_wide, wide_2, WIDTH)

    steps(lambda s, at: project_back(1, s, at))

    def bottom(s, at):
        gate = sigmoid(mixed[0, 4 * CH :, at])
        finish_back(
            0,
            s,
            at,
            upstream[:, at],
            norm_out[0, :, at],
            inverse_out[0, :, at],
            projected[0, :, at],
            gate,
        )

    steps(bottom)
    send_swap(6, send_slim, slim_3, 16)
    assemble_slim(6, slim_3, grad)
    result[0] = dot(right[0], grad[...], 1, 0)
    result[1] = dot(left[0], grad[...], 1, 1)
    split_wide(7, result.at[0], result.at[1], wide_3)
    receive_swap(7, send_wide, wide_3, WIDTH)

    steps(lambda s, at: project_back(0, s, at))
    store_block(upstream, flat)
    final = pltpu.make_async_copy(flat, grad_hbm, copy_sem.at[1])
    final.start()
    store.wait()
    final.wait()


def local(
    pair_input, chain_lengths, input_gain, input_weight, output_gain, output_weight, cotangent
):
    cells = HEIGHT * WIDTH
    vmem = pl.BlockSpec(memory_space=pltpu.VMEM)
    hbm = pl.BlockSpec(memory_space=pl.ANY)
    smem = pl.BlockSpec(memory_space=pltpu.SMEM)
    wide = pltpu.VMEM((DEVICES, WIDTH, 128), BF16)
    slim = pltpu.VMEM((DEVICES, 16, 128), BF16)
    plane = pltpu.VMEM((CH, LANES), F32)
    planes = pltpu.VMEM((2, CH, LANES), F32)
    line = pltpu.VMEM((2, 1, LANES), F32)
    out, grad = pl.pallas_call(
        kernel,
        out_shape=(
            jax.ShapeDtypeStruct((cells, CH), BF16),
            jax.ShapeDtypeStruct((cells, CH), F32),
        ),
        in_specs=[hbm, smem, vmem, hbm, vmem, hbm, hbm],
        out_specs=(hbm, hbm),
        scratch_shapes=[
            pltpu.VMEM((cells, CH), BF16),
            pltpu.VMEM((2, CH, 5 * CH), BF16),
            pltpu.VMEM((2, CH, CH), BF16),
            pltpu.VMEM((cells, CH), BF16),
            pltpu.VMEM((cells, CH), F32),
            plane,
            plane,
            pltpu.VMEM((2, 5 * CH, LANES), F32),
            planes,
            line,
            planes,
            line,
            planes,
            pltpu.VMEM((CH * WIDTH, 128), F32),
            pltpu.VMEM((CH * WIDTH, 128), F32),
            pltpu.VMEM((4, CH, STEP), F32),
            pltpu.VMEM((2, 5 * CH, CH), BF16),
            pltpu.VMEM((2, CH, CH), BF16),
            pltpu.VMEM((2, SIDE, SIDE), BF16),
            pltpu.VMEM((2, SIDE, SIDE), BF16),
            pltpu.VMEM((SIDE, SIDE), BF16),
            pltpu.VMEM((2, SIDE, SIDE), F32),
            wide,
            slim,
            wide,
            wide,
            wide,
            wide,
            slim,
            slim,
            slim,
            slim,
            pltpu.SemaphoreType.DMA((8,)),
            pltpu.SemaphoreType.DMA((8, CHAINS)),
            pltpu.SemaphoreType.DMA((4,)),
        ],
        compiler_params=pltpu.CompilerParams(
            collective_id=0, has_side_effects=True, vmem_limit_bytes=52 * 2**20
        ),
    )(
        pair_input.reshape(cells, CH),
        chain_lengths,
        input_gain,
        input_weight,
        output_gain,
        output_weight,
        cotangent.reshape(cells, CH),
    )
    shape = (HEIGHT, WIDTH, CH)
    return out.reshape(shape), grad.reshape(shape)


def solution(mesh):
    placed = (P("row", "col", None), P(), P(), P(), P(), P(), P("row", "col", None))
    return jax.shard_map(
        local,
        mesh=mesh,
        in_specs=placed,
        out_specs=(P("row", "col", None), P("row", "col", None)),
        check_vma=False,
    )
```

time: 148 us -> 132 us (0.89)
  Pallas kernels: 141 us -> 125 us
    pallas_call x1, Pallas kernels: 141 us -> 125 us  [local(): pl.pallas_call(kernel, out_shape=(jax.ShapeDtypeStruct((cells, CH), BF16)...]
where the time goes in v3:
time: 132 us
  Pallas kernels  125 us (95%)
  local copies, waits for them, and re-layouts  5.94 us (4%)
    pallas_call x1, Pallas kernels, local(): pl.pallas_call(kernel, out_shape=(jax.ShapeDtypeStruct((cells, CH), BF16)...  125 us
    unnamed x16, local copies, waits for them, and re-layouts  5.94 us

profile of v3, /device:TPU:1, one launch (start us, length us, event | category | flops | bytes accessed | tf_op | source)
XLA Modules:
  0.0 131.7 jit_solution(5458163769416144592)
XLA Ops:
  0.6 0.0 copy-start.5
  0.6 0.0 copy-start.4
  0.7 0.0 copy-start.6
  0.7 0.7 copy-done.5
  1.3 0.0 copy-done.4
  1.3 0.0 copy-done.6
  1.3 0.0 copy-start
  1.3 1.0 copy-done
  2.3 0.0 copy-start.1
  2.3 1.0 copy-done.1
  3.3 0.0 copy-start.2
  3.3 1.0 copy-done.2
  4.2 0.0 copy-start.3
  4.2 0.8 copy-done.3
  5.1 125.1 %shard_map.86 = (bf16[1152,128]{1,0:T(8,128)(2,1)S(1)}, f32[1152,128]{1,0:T(8,128)S(1)}) custom-call(bf16[1152,128]{1,0:T(8,128)(2,1)S(1)} %bitcast.5, s32[8]{0:T(128)S(1)} %copy-done.6, f32[2,128]{1,0:T(2,128)S(1)} %copy-done.4, bf16[2,128,640]{2,1,0:T(8,128)(2,1)S(1)} %copy-done, f32[2,128]{1,0:T(2,128)S(1)} %copy-done.5, ...), custom_call_target="tpu_custom_call" | custom-call | tf_op jit(solution)/shard_map/pallas_call | solution.py:503
  130.2 0.7 copy.11
  130.9 0.8 copy.12
Async XLA Ops:
  0.6 0.7 copy-start.5
  0.6 0.7 copy-start.4
  0.7 0.7 copy-start.6
  1.3 1.0 copy-start
  2.3 1.0 copy-start.1
  3.3 1.0 copy-start.2
  4.2 0.8 copy-start.3

commit v4 on v3

--- a/solution.py
+++ b/solution.py
@@ -122,6 +122,8 @@
     row, col = lax.axis_index("row"), lax.axis_index("col")
     me = row * COLS + col
     my_chain = col // 2
+    my_pair = row // 2
+    my_group = lax.rem(my_chain + 2 * (4 - my_pair), CHAINS)
 
     loads = [
         pltpu.make_async_copy(source, target, copy_sem.at[i])
@@ -141,37 +143,43 @@
 
     lax.fori_loop(1, DEVICES, greet, 0)
 
-    def send(phase, source, target, chain):
-        for step in range(ROWS):
-            for part in range(2):
-                peer = (lax.rem(row + step, ROWS), chain * 2 + part)
-                at = peer[0] * COLS + peer[1]
-
-                def start():
-                    pltpu.make_async_remote_copy(
-                        source.at[at],
-                        target.at[me],
-                        send_sem.at[phase],
-                        recv_sem.at[phase, my_chain],
-                        device_id=peer,
-                        device_id_type=MESH,
-                    ).start()
-
-                if step > 0:
-                    start()
-                else:
-
-                    @pl.when(at != me)
-                    def _():
+    def chain_of(group, pair):
+        return lax.rem(group + 2 * pair, CHAINS)
+
+    def send(phase, source, target, group):
+        for step in range(ROWS // 2):
+            pair = lax.rem(my_pair + step, ROWS // 2)
+            chain = chain_of(group, pair)
+            for low in range(2):
+                for part in range(2):
+                    peer = (pair * 2 + lax.rem(row + low, 2), chain * 2 + part)
+                    at = peer[0] * COLS + peer[1]
+
+                    def start(peer=peer, at=at):
+                        pltpu.make_async_remote_copy(
+                            source.at[at],
+                            target.at[me],
+                            send_sem.at[phase],
+                            recv_sem.at[phase, my_group],
+                            device_id=peer,
+                            device_id_type=MESH,
+                        ).start()
+
+                    if step + low > 0:
                         start()
-
-                    @pl.when(at == me)
-                    def _():
-                        target[me] = source[me]
+                    else:
+
+                        @pl.when(at != me)
+                        def _():
+                            start()
+
+                        @pl.when(at == me)
+                        def _():
+                            target[me] = source[me]
 
     def send_all(body):
         def one(s, carry):
-            body(lax.rem(my_chain + s, CHAINS))
+            body(lax.rem(my_group + s, CHAINS))
             return carry
 
         lax.fori_loop(0, CHAINS, one, 0)
@@ -183,13 +191,13 @@
                 source.at[some],
                 target.at[some],
                 send_sem.at[phase],
-                recv_sem.at[phase, my_chain],
+                recv_sem.at[phase, my_group],
                 device_id=(row, col),
                 device_id_type=MESH,
             )
 
         def one(s, carry):
-            chain = lax.rem(my_chain + CHAINS - s, CHAINS)
+            group = lax.rem(my_group + CHAINS - s, CHAINS)
 
             def wait(count):
                 some = pl.ds(0, count)
@@ -197,7 +205,7 @@
                     source.at[some],
                     target.at[some],
                     send_sem.at[phase],
-                    recv_sem.at[phase, chain],
+                    recv_sem.at[phase, group],
                     device_id=(row, col),
                     device_id_type=MESH,
                 ).wait_recv()
@@ -210,7 +218,7 @@
             def _():
                 wait(2 * ROWS)
 
-            body(chain)
+            body(group)
             return carry
 
         lax.fori_loop(0, CHAINS, one, 0)
@@ -221,7 +229,7 @@
             body(s, pl.ds(pl.multiple_of(s * STEP, STEP), STEP))
             return carry
 
-        lax.fori_loop(0, STEPS, one, 0)
+        lax.fori_loop(0, STEPS, one, 0, unroll=True)
 
     def tiles_of(s):
         pairs = []
@@ -276,29 +284,29 @@
 
     def put_slim(s, values):
         for i in range(2):
-            swap[pl.ds(s * 2 + i, CH, stride=16), :] = values[:, i * 128 : (i + 1) * 128]
+            swap[pl.ds(s * 2 + i, CH, stride=TILES), :] = values[:, i * 128 : (i + 1) * 128]
 
     def get_slim(s):
         return jnp.concatenate(
-            [inbox[pl.ds(s * 2 + i, CH, stride=16), :] for i in range(2)], axis=1
+            [inbox[pl.ds(s * 2 + i, CH, stride=TILES), :] for i in range(2)], axis=1
         )
 
-    def channels_of(chain, rows):
+    def channels_of(group, rows):
         for device_row in range(ROWS):
-            at = device_row * COLS + chain * 2
+            at = device_row * COLS + chain_of(group, device_row // 2) * 2
             yield pl.ds(at, 2), pl.ds(pl.multiple_of(at * rows, 2 * rows), 2 * rows)
 
     def send_swap(phase, source, target, rows):
-        def body(chain):
-            for messages, at in channels_of(chain, rows):
-                source[messages] = swap[at, :].astype(BF16).reshape(2, rows, 128)
-            send(phase, source, target, chain)
+        def body(group):
+            for messages, at in channels_of(group, rows):
+                source[messages] = swap[at, :].astype(BF16).reshape((2,) + source.shape[1:])
+            send(phase, source, target, group)
 
         send_all(body)
 
     def receive_swap(phase, source, target, rows):
-        def body(chain):
-            for messages, at in channels_of(chain, rows):
+        def body(group):
+            for messages, at in channels_of(group, rows):
                 inbox[at, :] = target[messages].astype(F32).reshape(2 * rows, 128)
 
         receive(phase, source, target, body)
@@ -349,17 +357,18 @@
         upstream[:, at] = after
         return after
 
-    def places(chain):
-        down = pl.ds(pl.multiple_of(chain * HALF, HALF), HALF)
+    def places(group):
         for pair in range(ROWS // 2):
+            chain = chain_of(group, pair)
+            down = pl.ds(pl.multiple_of(chain * HALF, HALF), HALF)
             indices = [pair * 2 * COLS + chain * 2 + part for part in range(2)]
             yield down, slice(pair * 128, (pair + 1) * 128), indices
 
     empty = jnp.zeros((HALF - 2 * WIDTH, 128), F32)
 
     def assemble_wide(phase, source, first, second):
-        def body(chain):
-            for down, across, indices in places(chain):
+        def body(group):
+            for down, across, indices in places(group):
                 firsts, seconds = [], []
                 for at in indices:
                     one, two = merge(source[at].astype(F32), source[at + COLS].astype(F32))
@@ -370,13 +379,17 @@
 
         receive(phase, send_wide, source, body)
 
+    def open_slim(source, at):
+        rows = source[at].astype(F32).reshape(TILES, 128)
+        return jnp.concatenate([rows, jnp.zeros((4, 128), F32)], axis=0)
+
     def assemble_slim(phase, source, target):
-        def body(chain):
+        def body(group):
             low = lax.broadcasted_iota(jnp.int32, (8, 128), 0) < 4
-            for down, across, indices in places(chain):
+            for down, across, indices in places(group):
                 parts = []
                 for at in indices:
-                    one, two = merge(source[at].astype(F32), source[at + COLS].astype(F32))
+                    one, two = merge(open_slim(source, at), open_slim(source, at + COLS))
                     last = jnp.where(low, one[8:16], pltpu.roll(two[8:16], 4, axis=0))
                     parts += [one[0:8], two[0:8], last]
                 target[down, across] = jnp.concatenate(parts + [empty], axis=0).astype(BF16)
@@ -384,29 +397,30 @@
         receive(phase, send_slim, source, body)
 
     def split_wide(phase, first, second, target):
-        def body(chain):
-            for down, across, indices in places(chain):
+        def body(group):
+            for down, across, indices in places(group):
                 lower, upper = merge(first[down, across], second[down, across])
                 for part, at in enumerate(indices):
                     cut = slice(part * WIDTH, (part + 1) * WIDTH)
                     send_wide[at] = lower[cut].astype(BF16)
                     send_wide[at + COLS] = upper[cut].astype(BF16)
-            send(phase, send_wide, target, chain)
+            send(phase, send_wide, target, group)
 
         send_all(body)
 
     def split_slim(phase, source, target):
-        def body(chain):
-            for down, across, indices in places(chain):
+        def body(group):
+            for down, across, indices in places(group):
                 values = source[down, across]
                 for part, at in enumerate(indices):
                     cut = values[part * WIDTH : (part + 1) * WIDTH]
                     last = cut[16:24]
                     low_0, low_1 = merge(cut[0:8], cut[8:16])
                     high_0, high_1 = merge(last, pltpu.roll(last, 4, axis=0))
-                    send_slim[at] = jnp.concatenate([low_0, high_0], axis=0).astype(BF16)
-                    send_slim[at + COLS] = jnp.concatenate([low_1, high_1], axis=0).astype(BF16)
-            send(phase, send_slim, target, chain)
+                    for to, lines in ((at, (low_0, high_0)), (at + COLS, (low_1, high_1))):
+                        rows = jnp.concatenate([lines[0], lines[1][0:4]], axis=0)
+                        send_slim[to] = rows.astype(BF16).reshape(3, 4, 128)
+            send(phase, send_slim, target, group)
 
         send_all(body)
 
@@ -429,7 +443,7 @@
     assemble_wide(0, wide_0, left.at[0], right.at[0])
     result[0] = dot(right[0], left[0], 0, 0)
     split_slim(1, result.at[0], slim_0)
-    receive_swap(1, send_slim, slim_0, 16)
+    receive_swap(1, send_slim, slim_0, TILES)
 
     def middle(s, at):
         project(1, s, at, finish(0, s, at)[0])
@@ -439,14 +453,14 @@
     assemble_wide(2, wide_1, left.at[1], right.at[1])
     result[0] = dot(right[1], left[1], 1, 1)
     split_slim(3, result.at[0], slim_1)
-    receive_swap(3, send_slim, slim_1, 16)
+    receive_swap(3, send_slim, slim_1, TILES)
 
     def top(s, at):
         _, normed, inverse, values, gate = finish(1, s, at)
         finish_back(1, s, at, upstream[:, at], normed, inverse, values, gate)
 
     steps(top)
-    send_swap(4, send_slim, slim_2, 16)
+    send_swap(4, send_slim, slim_2, TILES)
     store_block(state, flat)
     block[...] = flat[...].astype(BF16)
     store = pltpu.make_async_copy(block, out_hbm, copy_sem.at[0])
@@ -473,7 +487,7 @@
         )
 
     steps(bottom)
-    send_swap(6, send_slim, slim_3, 16)
+    send_swap(6, send_slim, slim_3, TILES)
     assemble_slim(6, slim_3, grad)
     result[0] = dot(right[0], grad[...], 1, 0)
     result[1] = dot(left[0], grad[...], 1, 1)
@@ -496,7 +510,7 @@
     hbm = pl.BlockSpec(memory_space=pl.ANY)
     smem = pl.BlockSpec(memory_space=pltpu.SMEM)
     wide = pltpu.VMEM((DEVICES, WIDTH, 128), BF16)
-    slim = pltpu.VMEM((DEVICES, 16, 128), BF16)
+    slim = pltpu.VMEM((DEVICES, 3, 4, 128), BF16)
     plane = pltpu.VMEM((CH, LANES), F32)
     planes = pltpu.VMEM((2, CH, LANES), F32)
     line = pltpu.VMEM((2, 1, LANES), F32)

time: 132 us -> 118 us (0.89)
  Pallas kernels: 125 us -> 111 us
    pallas_call x1, Pallas kernels: 125 us -> 111 us  [local(): pl.pallas_call(kernel, out_shape=(jax.ShapeDtypeStruct((cells, CH), BF16)...]
where the time goes in v4:
time: 118 us; the launch traced here: 117 us
  Pallas kernels  111 us (94%)
  local copies, waits for them, and re-layouts  5.94 us (5%)
    pallas_call x1, Pallas kernels, local(): pl.pallas_call(kernel, out_shape=(jax.ShapeDtypeStruct((cells, CH), BF16)...  111 us
    unnamed x16, local copies, waits for them, and re-layouts  5.94 us

profile of v4, /device:TPU:1, one launch (start us, length us, event | category | flops | bytes accessed | tf_op | source)
XLA Modules:
  0.0 117.3 jit_solution(3297633148693656680)
XLA Ops:
  0.6 0.0 copy-start.5
  0.6 0.0 copy-start.4
  0.7 0.0 copy-start.6
  0.7 0.7 copy-done.5
  1.3 0.0 copy-done.4
  1.3 0.0 copy-done.6
  1.3 0.0 copy-start
  1.3 1.0 copy-done
  2.3 0.0 copy-start.1
  2.3 1.0 copy-done.1
  3.3 0.0 copy-start.2
  3.3 1.0 copy-done.2
  4.2 0.0 copy-start.3
  4.2 0.8 copy-done.3
  5.1 110.7 %shard_map.86 = (bf16[1152,128]{1,0:T(8,128)(2,1)S(1)}, f32[1152,128]{1,0:T(8,128)S(1)}) custom-call(bf16[1152,128]{1,0:T(8,128)(2,1)S(1)} %bitcast.5, s32[8]{0:T(128)S(1)} %copy-done.6, f32[2,128]{1,0:T(2,128)S(1)} %copy-done.4, bf16[2,128,640]{2,1,0:T(8,128)(2,1)S(1)} %copy-done, f32[2,128]{1,0:T(2,128)S(1)} %copy-done.5, ...), custom_call_target="tpu_custom_call" | custom-call | tf_op jit(solution)/shard_map/pallas_call | solution.py:517
  115.8 0.7 copy.11
  116.5 0.8 copy.12
Async XLA Ops:
  0.6 0.7 copy-start.5
  0.6 0.7 copy-start.4
  0.7 0.7 copy-start.6
  1.3 1.0 copy-start
  2.3 1.0 copy-start.1
  3.3 1.0 copy-start.2
  4.2 0.8 copy-start.3

commit v5 on v4

--- a/solution.py
+++ b/solution.py
@@ -25,6 +25,14 @@
 STEP = 256
 STEPS = LANES // STEP
 SIDE = CHAINS * HALF
+
+
+UNITS = (
+    (20842, 2390, 4165),
+    (64490, 1022, 4164),
+    (325, 6122, 17489),
+    (1007, 15690, 1105),
+)
 
 
 def column_pair(tile):
@@ -96,6 +104,7 @@
     norm_out,
     inverse_out,
     projected,
+    early_back,
     swap,
     inbox,
     gains,
@@ -123,7 +132,6 @@
     me = row * COLS + col
     my_chain = col // 2
     my_pair = row // 2
-    my_group = lax.rem(my_chain + 2 * (4 - my_pair), CHAINS)
 
     loads = [
         pltpu.make_async_copy(source, target, copy_sem.at[i])
@@ -136,20 +144,20 @@
 
     barrier = pltpu.get_barrier_semaphore()
 
-    def greet(t, carry):
-        peer = (lax.rem(row + t // COLS, ROWS), lax.rem(col + t % COLS, COLS))
-        pl.semaphore_signal(barrier, inc=1, device_id=peer, device_id_type=MESH)
-        return carry
-
-    lax.fori_loop(1, DEVICES, greet, 0)
-
-    def chain_of(group, pair):
-        return lax.rem(group + 2 * pair, CHAINS)
+    def greet(first, last):
+        for t in range(first, last):
+            peer = (lax.rem(row + t // COLS, ROWS), lax.rem(col + t % COLS, COLS))
+            pl.semaphore_signal(barrier, inc=1, device_id=peer, device_id_type=MESH)
+
+    def units_of(group, sign):
+        for offsets in UNITS:
+            x, z, y = [(bits >> (2 * group)) & 3 for bits in offsets]
+            pair = (my_pair + sign * z) & 3
+            chain = ((my_chain // 2 + sign * x) & 3) * 2 + (my_chain + y) % 2
+            yield pair, chain
 
     def send(phase, source, target, group):
-        for step in range(ROWS // 2):
-            pair = lax.rem(my_pair + step, ROWS // 2)
-            chain = chain_of(group, pair)
+        for unit, (pair, chain) in enumerate(units_of(group, 1)):
             for low in range(2):
                 for part in range(2):
                     peer = (pair * 2 + lax.rem(row + low, 2), chain * 2 + part)
@@ -160,12 +168,12 @@
                             source.at[at],
                             target.at[me],
                             send_sem.at[phase],
-                            recv_sem.at[phase, my_group],
+                            recv_sem.at[phase, group],
                             device_id=peer,
                             device_id_type=MESH,
                         ).start()
 
-                    if step + low > 0:
+                    if unit < 3 or low > 0:
                         start()
                     else:
 
@@ -179,7 +187,7 @@
 
     def send_all(body):
         def one(s, carry):
-            body(lax.rem(my_group + s, CHAINS))
+            body(s)
             return carry
 
         lax.fori_loop(0, CHAINS, one, 0)
@@ -191,14 +199,12 @@
                 source.at[some],
                 target.at[some],
                 send_sem.at[phase],
-                recv_sem.at[phase, my_group],
+                recv_sem.at[phase, 0],
                 device_id=(row, col),
                 device_id_type=MESH,
             )
 
-        def one(s, carry):
-            group = lax.rem(my_group + CHAINS - s, CHAINS)
-
+        def one(group, carry):
             def wait(count):
                 some = pl.ds(0, count)
                 pltpu.make_async_remote_copy(
@@ -210,11 +216,11 @@
                     device_id_type=MESH,
                 ).wait_recv()
 
-            @pl.when(s == 0)
+            @pl.when(group == CHAINS - 1)
             def _():
                 wait(2 * ROWS - 1)
 
-            @pl.when(s > 0)
+            @pl.when(group < CHAINS - 1)
             def _():
                 wait(2 * ROWS)
 
@@ -248,7 +254,7 @@
         inside = (token < length_ref[row]) & (column < length_ref[my_chain])
         return jnp.where(inside, 1.0, 0.0)
 
-    def load_block(source, target):
+    def load_block(source, target, beside=lambda tile: None):
         flat[...] = source[...].astype(F32)
         empty = jnp.zeros((HALF - HEIGHT, CH), F32)
         for tile in range(TILES):
@@ -256,6 +262,7 @@
             for column in column_pair(tile):
                 parts += [flat[pl.ds(column, HEIGHT, stride=WIDTH), :], empty]
             target[:, tile * 128 : (tile + 1) * 128] = jnp.concatenate(parts, axis=0).T
+            beside(tile)
 
     def store_block(source, target):
         for tile in range(TILES):
@@ -291,14 +298,15 @@
             [inbox[pl.ds(s * 2 + i, CH, stride=TILES), :] for i in range(2)], axis=1
         )
 
-    def channels_of(group, rows):
-        for device_row in range(ROWS):
-            at = device_row * COLS + chain_of(group, device_row // 2) * 2
-            yield pl.ds(at, 2), pl.ds(pl.multiple_of(at * rows, 2 * rows), 2 * rows)
+    def channels_of(group, sign, rows):
+        for pair, chain in units_of(group, sign):
+            for low in range(2):
+                at = (pair * 2 + low) * COLS + chain * 2
+                yield pl.ds(at, 2), pl.ds(pl.multiple_of(at * rows, 2 * rows), 2 * rows)
 
     def send_swap(phase, source, target, rows):
         def body(group):
-            for messages, at in channels_of(group, rows):
+            for messages, at in channels_of(group, 1, rows):
                 source[messages] = swap[at, :].astype(BF16).reshape((2,) + source.shape[1:])
             send(phase, source, target, group)
 
@@ -306,7 +314,7 @@
 
     def receive_swap(phase, source, target, rows):
         def body(group):
-            for messages, at in channels_of(group, rows):
+            for messages, at in channels_of(group, -1, rows):
                 inbox[at, :] = target[messages].astype(F32).reshape(2 * rows, 128)
 
         receive(phase, source, target, body)
@@ -330,25 +338,40 @@
         inverse_out[u, :, at] = inverse
         values = dot(out_weight_t[u], (normed * gains[2 + u]).astype(BF16))
         projected[u, :, at] = values
-        gate = sigmoid(mixed[u, 4 * CH :, at])
+        gate = mixed[u, 4 * CH :, at]
         after = (state[:, at] + gate * values).astype(BF16).astype(F32)
         state[:, at] = after
         return after, normed, inverse, values, gate
 
-    def finish_back(u, s, at, up, normed, inverse, values, gate):
+    def scaled_back(u, at, grad_projected):
+        return dot(ow_ref[u], grad_projected.astype(BF16)) * gains[2 + u]
+
+    def early(s, at):
+        early_back[:, at] = scaled_back(1, at, upstream[:, at] * mixed[1, 4 * CH :, at])
+
+    def finish_back(u, s, at, up, normed, inverse, values, gate, grad_scaled=None):
         grad_projected = up * gate
         mixed[u, 4 * CH :, at] = grad_projected * values * (1.0 - gate)
-        grad_scaled = dot(ow_ref[u], grad_projected.astype(BF16))
-        put_slim(s, norm_backward(grad_scaled * gains[2 + u], normed, inverse))
+        if grad_scaled is None:
+            grad_scaled = scaled_back(u, at, grad_projected)
+        put_slim(s, norm_backward(grad_scaled, normed, inverse))
+
+    def gates(u, s, at):
+        mixed[u, 4 * CH :, at] = sigmoid(mixed[u, 4 * CH :, at])
+
+    def factors(u, s, at):
+        keep = valid(s)
+        for base in (0, 2 * CH):
+            gate = sigmoid(mixed[u, base + CH : base + 2 * CH, at])
+            kept = gate * keep
+            mixed[u, base : base + CH, at] = mixed[u, base : base + CH, at] * kept * (1.0 - gate)
+            mixed[u, base + CH : base + 2 * CH, at] = kept
 
     def project_back(u, s, at):
-        keep = valid(s)
         parts = []
         for values, base in zip(get_wide(s), (0, 2 * CH)):
-            gate = sigmoid(mixed[u, base + CH : base + 2 * CH, at])
-            direct = values * gate * keep
-            parts.append(direct.astype(BF16))
-            parts.append((direct * mixed[u, base : base + CH, at] * (1.0 - gate)).astype(BF16))
+            parts.append((values * mixed[u, base + CH : base + 2 * CH, at]).astype(BF16))
+            parts.append((values * mixed[u, base : base + CH, at]).astype(BF16))
         parts.append(mixed[u, 4 * CH :, at].astype(BF16))
         grad_scaled = dot(iw_ref[u], jnp.concatenate(parts, axis=0))
         after = upstream[:, at] + norm_backward(
@@ -357,18 +380,19 @@
         upstream[:, at] = after
         return after
 
-    def places(group):
-        for pair in range(ROWS // 2):
-            chain = chain_of(group, pair)
-            down = pl.ds(pl.multiple_of(chain * HALF, HALF), HALF)
-            indices = [pair * 2 * COLS + chain * 2 + part for part in range(2)]
-            yield down, slice(pair * 128, (pair + 1) * 128), indices
+    def places(group, sign):
+        for pair, chain in units_of(group, sign):
+            yield (
+                pl.ds(pl.multiple_of(chain * HALF, HALF), HALF),
+                pl.ds(pl.multiple_of(pair * 128, 128), 128),
+                [pair * 2 * COLS + chain * 2 + part for part in range(2)],
+            )
 
     empty = jnp.zeros((HALF - 2 * WIDTH, 128), F32)
 
     def assemble_wide(phase, source, first, second):
         def body(group):
-            for down, across, indices in places(group):
+            for down, across, indices in places(group, -1):
                 firsts, seconds = [], []
                 for at in indices:
                     one, two = merge(source[at].astype(F32), source[at + COLS].astype(F32))
@@ -386,7 +410,7 @@
     def assemble_slim(phase, source, target):
         def body(group):
             low = lax.broadcasted_iota(jnp.int32, (8, 128), 0) < 4
-            for down, across, indices in places(group):
+            for down, across, indices in places(group, -1):
                 parts = []
                 for at in indices:
                     one, two = merge(open_slim(source, at), open_slim(source, at + COLS))
@@ -398,7 +422,7 @@
 
     def split_wide(phase, first, second, target):
         def body(group):
-            for down, across, indices in places(group):
+            for down, across, indices in places(group, 1):
                 lower, upper = merge(first[down, across], second[down, across])
                 for part, at in enumerate(indices):
                     cut = slice(part * WIDTH, (part + 1) * WIDTH)
@@ -410,7 +434,7 @@
 
     def split_slim(phase, source, target):
         def body(group):
-            for down, across, indices in places(group):
+            for down, across, indices in places(group, 1):
                 values = source[down, across]
                 for part, at in enumerate(indices):
                     cut = values[part * WIDTH : (part + 1) * WIDTH]
@@ -424,25 +448,31 @@
 
         send_all(body)
 
+    greet(1, 30)
     loads[0].wait()
-    load_block(block, state)
-    loads[1].wait()
-    loads[2].wait()
-    for u in range(2):
+    load_block(block, state, lambda tile: greet(30 + tile * 8, 38 + tile * 8))
+    greet(126, DEVICES)
+    def prepare(u):
         weight_t[u] = iw_ref[u].astype(F32).T.astype(BF16)
         out_weight_t[u] = ow_ref[u].astype(F32).T.astype(BF16)
         for i, ref in ((u, ig_ref), (2 + u, og_ref)):
             spread = jnp.broadcast_to(ref[u : u + 1, :], (CH, CH)).T
             gains[i] = jnp.concatenate([spread, spread], axis=1)
 
+    loads[1].wait()
+    loads[2].wait()
+    prepare(0)
     steps(lambda s, at: project(0, s, at, state[:, at]))
     pl.semaphore_wait(barrier, DEVICES - 1)
     send_swap(0, send_wide, wide_0, WIDTH)
+    prepare(1)
     loads[3].wait()
     load_block(ct_ref, upstream)
     assemble_wide(0, wide_0, left.at[0], right.at[0])
     result[0] = dot(right[0], left[0], 0, 0)
     split_slim(1, result.at[0], slim_0)
+    steps(lambda s, at: gates(0, s, at))
+    steps(lambda s, at: factors(0, s, at))
     receive_swap(1, send_slim, slim_0, TILES)
 
     def middle(s, at):
@@ -450,14 +480,17 @@
 
     steps(middle)
     send_swap(2, send_wide, wide_1, WIDTH)
+    steps(lambda s, at: gates(1, s, at))
+    steps(early)
     assemble_wide(2, wide_1, left.at[1], right.at[1])
     result[0] = dot(right[1], left[1], 1, 1)
     split_slim(3, result.at[0], slim_1)
+    steps(lambda s, at: factors(1, s, at))
     receive_swap(3, send_slim, slim_1, TILES)
 
     def top(s, at):
         _, normed, inverse, values, gate = finish(1, s, at)
-        finish_back(1, s, at, upstream[:, at], normed, inverse, values, gate)
+        finish_back(1, s, at, upstream[:, at], normed, inverse, values, gate, early_back[:, at])
 
     steps(top)
     send_swap(4, send_slim, slim_2, TILES)
@@ -471,15 +504,14 @@
     split_wide(5, result.at[0], result.at[1], wide_2)
     receive_swap(5, send_wide, wide_2, WIDTH)
 
-    steps(lambda s, at: project_back(1, s, at))
-
     def bottom(s, at):
-        gate = sigmoid(mixed[0, 4 * CH :, at])
+        up = project_back(1, s, at)
+        gate = mixed[0, 4 * CH :, at]
         finish_back(
             0,
             s,
             at,
-            upstream[:, at],
+            up,
             norm_out[0, :, at],
             inverse_out[0, :, at],
             projected[0, :, at],
@@ -507,7 +539,8 @@
 ):
     cells = HEIGHT * WIDTH
     vmem = pl.BlockSpec(memory_space=pltpu.VMEM)
-    hbm = pl.BlockSpec(memory_space=pl.ANY)
+    hbm = pl.BlockSpec(memory_space=pltpu.HBM)
+    free = pl.BlockSpec(memory_space=pl.ANY)
     smem = pl.BlockSpec(memory_space=pltpu.SMEM)
     wide = pltpu.VMEM((DEVICES, WIDTH, 128), BF16)
     slim = pltpu.VMEM((DEVICES, 3, 4, 128), BF16)
@@ -521,7 +554,7 @@
             jax.ShapeDtypeStruct((cells, CH), F32),
         ),
         in_specs=[hbm, smem, vmem, hbm, vmem, hbm, hbm],
-        out_specs=(hbm, hbm),
+        out_specs=(free, free),
         scratch_shapes=[
             pltpu.VMEM((cells, CH), BF16),
             pltpu.VMEM((2, CH, 5 * CH), BF16),
@@ -536,6 +569,7 @@
             planes,
             line,
             planes,
+            plane,
             pltpu.VMEM((CH * WIDTH, 128), F32),
             pltpu.VMEM((CH * WIDTH, 128), F32),
             pltpu.VMEM((4, CH, STEP), F32),

time: 118 us -> 111 us (0.941)
  Pallas kernels: 111 us -> 104 us
    pallas_call x1, Pallas kernels: 111 us -> 104 us  [local(): pl.pallas_call(kernel, out_shape=(jax.ShapeDtypeStruct((cells, CH), BF16)...]
where the time goes in v5:
time: 111 us; the launch traced here: 110 us
  Pallas kernels  104 us (94%)
  local copies, waits for them, and re-layouts  5.94 us (5%)
    pallas_call x1, Pallas kernels, local(): pl.pallas_call(kernel, out_shape=(jax.ShapeDtypeStruct((cells, CH), BF16)...  104 us
    unnamed x16, local copies, waits for them, and re-layouts  5.94 us

profile of v5, /device:TPU:1, one launch (start us, length us, event | category | flops | bytes accessed | tf_op | source)
XLA Modules:
  0.0 110.5 jit_solution(10809009131351752910)
XLA Ops:
  0.6 0.0 copy-start.5
  0.6 0.0 copy-start.4
  0.7 0.0 copy-start.6
  0.7 0.7 copy-done.5
  1.3 0.0 copy-done.4
  1.3 0.0 copy-done.6
  1.3 0.0 copy-start
  1.3 1.0 copy-done
  2.3 0.0 copy-start.1
  2.3 1.0 copy-done.1
  3.3 0.0 copy-start.2
  3.3 1.0 copy-done.2
  4.2 0.0 copy-start.3
  4.2 0.8 copy-done.3
  5.1 103.9 %shard_map.86 = (bf16[1152,128]{1,0:T(8,128)(2,1)S(1)}, f32[1152,128]{1,0:T(8,128)S(1)}) custom-call(bf16[1152,128]{1,0:T(8,128)(2,1)S(1)} %bitcast.5, s32[8]{0:T(128)S(1)} %copy-done.6, f32[2,128]{1,0:T(2,128)S(1)} %copy-done.4, bf16[2,128,640]{2,1,0:T(8,128)(2,1)S(1)} %copy-done, f32[2,128]{1,0:T(2,128)S(1)} %copy-done.5, ...), custom_call_target="tpu_custom_call" | custom-call | tf_op jit(solution)/shard_map/pallas_call | solution.py:550
  108.9 0.7 copy.11
  109.6 0.8 copy.12
Async XLA Ops:
  0.6 0.7 copy-start.5
  0.6 0.7 copy-start.4
  0.7 0.7 copy-start.6
  1.3 1.0 copy-start
  2.3 1.0 copy-start.1
  3.3 1.0 copy-start.2
  4.2 0.8 copy-start.3

commit v6 on v5

--- a/solution.py
+++ b/solution.py
@@ -71,6 +71,39 @@
 
 def lower_lanes(shape):
     return lax.broadcasted_iota(jnp.int32, shape, len(shape) - 1) % 128 < HALF
+
+
+def half_lane():
+    return lax.broadcasted_iota(jnp.int32, (8, 128), 1) % HALF
+
+
+def upper_rows():
+    return lax.broadcasted_iota(jnp.int32, (8, 128), 0) < 4
+
+
+def fold(values):
+    first, second, last = values[0:8], values[8:16], values[16:24]
+    spare, low = half_lane() >= HEIGHT, upper_rows()
+    turned = pltpu.roll(last, 4, axis=0)
+    extra = jnp.where(low, pltpu.roll(turned, 48, axis=1), pltpu.roll(last, 32, axis=1))
+    first = jnp.where(spare, extra, first)
+    second = jnp.where(spare & low, pltpu.roll(turned, 16, axis=1), second)
+    return jnp.concatenate([first, second, last[0:4]], axis=0)
+
+
+def unfold(values):
+    first, second = values[0:8], values[8:16]
+    lane, low = half_lane(), upper_rows()
+    ends = jnp.where(lane < 16, pltpu.roll(first, 80, axis=1), pltpu.roll(second, 112, axis=1))
+    middle = (lane >= 16) & (lane < 32)
+    last = jnp.where(middle, pltpu.roll(first, 96, axis=1), pltpu.roll(ends, 4, axis=0))
+    kept = lane < HEIGHT
+    last = jnp.where(kept, last, 0.0)
+    held = jnp.concatenate([values[16:20], jnp.zeros((4, 128), F32)], axis=0)
+    return jnp.concatenate(
+        [jnp.where(kept, first, 0.0), jnp.where(kept, second, 0.0), jnp.where(low, held, last)],
+        axis=0,
+    )
 
 
 def merge(first, second):
@@ -304,10 +337,21 @@
                 at = (pair * 2 + low) * COLS + chain * 2
                 yield pl.ds(at, 2), pl.ds(pl.multiple_of(at * rows, 2 * rows), 2 * rows)
 
+    def put_folded(target, at, values):
+        target[at] = fold(values).astype(BF16).reshape(5, 4, 128)
+
+    def get_folded(source, at):
+        return unfold(source[at].astype(F32).reshape(20, 128))
+
     def send_swap(phase, source, target, rows):
         def body(group):
             for messages, at in channels_of(group, 1, rows):
-                source[messages] = swap[at, :].astype(BF16).reshape((2,) + source.shape[1:])
+                if rows == WIDTH:
+                    values = swap[at, :]
+                    for i in range(2):
+                        put_folded(source, messages.start + i, values[i * rows : (i + 1) * rows])
+                else:
+                    source[messages] = swap[at, :].astype(BF16).reshape((2,) + source.shape[1:])
             send(phase, source, target, group)
 
         send_all(body)
@@ -315,7 +359,11 @@
     def receive_swap(phase, source, target, rows):
         def body(group):
             for messages, at in channels_of(group, -1, rows):
-                inbox[at, :] = target[messages].astype(F32).reshape(2 * rows, 128)
+                if rows == WIDTH:
+                    parts = [get_folded(target, messages.start + i) for i in range(2)]
+                    inbox[at, :] = jnp.concatenate(parts, axis=0)
+                else:
+                    inbox[at, :] = target[messages].astype(F32).reshape(2 * rows, 128)
 
         receive(phase, source, target, body)
 
@@ -395,7 +443,7 @@
             for down, across, indices in places(group, -1):
                 firsts, seconds = [], []
                 for at in indices:
-                    one, two = merge(source[at].astype(F32), source[at + COLS].astype(F32))
+                    one, two = merge(get_folded(source, at), get_folded(source, at + COLS))
                     firsts.append(one)
                     seconds.append(two)
                 first[down, across] = jnp.concatenate(firsts + [empty], axis=0).astype(BF16)
@@ -426,8 +474,8 @@
                 lower, upper = merge(first[down, across], second[down, across])
                 for part, at in enumerate(indices):
                     cut = slice(part * WIDTH, (part + 1) * WIDTH)
-                    send_wide[at] = lower[cut].astype(BF16)
-                    send_wide[at + COLS] = upper[cut].astype(BF16)
+                    put_folded(send_wide, at, lower[cut])
+                    put_folded(send_wide, at + COLS, upper[cut])
             send(phase, send_wide, target, group)
 
         send_all(body)
@@ -542,7 +590,7 @@
     hbm = pl.BlockSpec(memory_space=pltpu.HBM)
     free = pl.BlockSpec(memory_space=pl.ANY)
     smem = pl.BlockSpec(memory_space=pltpu.SMEM)
-    wide = pltpu.VMEM((DEVICES, WIDTH, 128), BF16)
+    wide = pltpu.VMEM((DEVICES, 5, 4, 128), BF16)
     slim = pltpu.VMEM((DEVICES, 3, 4, 128), BF16)
     plane = pltpu.VMEM((CH, LANES), F32)
     planes = pltpu.VMEM((2, CH, LANES), F32)
@@ -594,7 +642,7 @@
             pltpu.SemaphoreType.DMA((4,)),
         ],
         compiler_params=pltpu.CompilerParams(
-            collective_id=0, has_side_effects=True, vmem_limit_bytes=52 * 2**20
+            collective_id=0, has_side_effects=True, vmem_limit_bytes=64 * 2**20 - 64 * 2**10
         ),
     )(
         pair_input.reshape(cells, CH),

time: 111 us -> 105 us (0.946)
  local copies, waits for them, and re-layouts: 5.94 us -> 2.58 us
  Pallas kernels: 104 us -> 102 us
    unnamed x16 -> x4, local copies, waits for them, and re-layouts: 5.94 us -> 2.58 us
    pallas_call x1, Pallas kernels: 104 us -> 102 us  [local(): pl.pallas_call(kernel, out_shape=(jax.ShapeDtypeStruct((cells, CH), BF16)...]
where the time goes in v6:
time: 105 us
  Pallas kernels  102 us (97%)
  local copies, waits for them, and re-layouts  2.58 us (2%)
    pallas_call x1, Pallas kernels, local(): pl.pallas_call(kernel, out_shape=(jax.ShapeDtypeStruct((cells, CH), BF16)...  102 us
    unnamed x4, local copies, waits for them, and re-layouts  2.58 us

profile of v6, /device:TPU:1, one launch (start us, length us, event | category | flops | bytes accessed | tf_op | source)
XLA Modules:
  0.0 105.3 jit_solution(7203626463287889294)
XLA Ops:
  0.6 102.1 %shard_map.86 = (bf16[1152,128]{1,0:T(8,128)(2,1)}, f32[1152,128]{1,0:T(8,128)}) custom-call(bf16[1152,128]{1,0:T(8,128)(2,1)} %bitcast.5, s32[8]{0:T(128)} %length_ref.1, f32[2,128]{1,0:T(2,128)} %ig_ref.1, bf16[2,128,640]{2,1,0:T(8,128)(2,1)} %iw_hbm.1, f32[2,128]{1,0:T(2,128)} %og_ref.1, bf16[2,128,128]{2,1,0:T(8,128)(2,1)} %ow_hbm.1, ...), custom_call_target="tpu_custom_call" | custom-call | tf_op jit(solution)/shard_map/pallas_call | solution.py:598
  102.7 0.0 copy-start
  102.7 1.8 %copy.11 = bf16[48,24,128]{2,1,0:T(8,128)(2,1)} copy(bf16[48,24,128]{2,1,0:T(8,128)(2,1)} %bitcast.7) | data formatting | bytes 589824
  104.5 0.0 copy-done
  104.5 0.8 copy.12
Async XLA Ops:
  102.7 1.8 %copy-start = (f32[1152,128]{1,0:T(8,128)S(1)}, f32[1152,128]{1,0:T(8,128)}, u32[]{:S(2)}) copy-start(f32[1152,128]{1,0:T(8,128)} %get-tuple-element.5) | copy-start | bytes 1769476

commit v7 on v6

--- a/solution.py
+++ b/solution.py
@@ -33,6 +33,13 @@
     (325, 6122, 17489),
     (1007, 15690, 1105),
 )
+
+
+def distance(offset):
+    return -min(offset[0], ROWS - offset[0]) / 2 - min(offset[1], COLS - offset[1]) / 4
+
+
+FAR_FIRST = sorted(((t // COLS, t % COLS) for t in range(DEVICES)), key=distance)
 
 
 def column_pair(tile):
@@ -179,7 +186,8 @@
 
     def greet(first, last):
         for t in range(first, last):
-            peer = (lax.rem(row + t // COLS, ROWS), lax.rem(col + t % COLS, COLS))
+            down, across = FAR_FIRST[t]
+            peer = (lax.rem(row + down, ROWS), lax.rem(col + across, COLS))
             pl.semaphore_signal(barrier, inc=1, device_id=peer, device_id_type=MESH)
 
     def units_of(group, sign):
@@ -496,10 +504,7 @@
 
         send_all(body)
 
-    greet(1, 30)
-    loads[0].wait()
-    load_block(block, state, lambda tile: greet(30 + tile * 8, 38 + tile * 8))
-    greet(126, DEVICES)
+    greet(0, 40)
     def prepare(u):
         weight_t[u] = iw_ref[u].astype(F32).T.astype(BF16)
         out_weight_t[u] = ow_ref[u].astype(F32).T.astype(BF16)
@@ -510,6 +515,9 @@
     loads[1].wait()
     loads[2].wait()
     prepare(0)
+    greet(40, 67)
+    loads[0].wait()
+    load_block(block, state, lambda tile: greet(67 + tile * 5, 72 + tile * 5))
     steps(lambda s, at: project(0, s, at, state[:, at]))
     pl.semaphore_wait(barrier, DEVICES - 1)
     send_swap(0, send_wide, wide_0, WIDTH)
@@ -543,8 +551,7 @@
     steps(top)
     send_swap(4, send_slim, slim_2, TILES)
     store_block(state, flat)
-    block[...] = flat[...].astype(BF16)
-    store = pltpu.make_async_copy(block, out_hbm, copy_sem.at[0])
+    store = pltpu.make_async_copy(flat, out_hbm, copy_sem.at[0])
     store.start()
     assemble_slim(4, slim_2, grad)
     result[0] = dot(grad[...], right[1], 0, 0)
@@ -575,10 +582,10 @@
     receive_swap(7, send_wide, wide_3, WIDTH)
 
     steps(lambda s, at: project_back(0, s, at))
+    store.wait()
     store_block(upstream, flat)
     final = pltpu.make_async_copy(flat, grad_hbm, copy_sem.at[1])
     final.start()
-    store.wait()
     final.wait()
 
 
@@ -598,7 +605,7 @@
     out, grad = pl.pallas_call(
         kernel,
         out_shape=(
-            jax.ShapeDtypeStruct((cells, CH), BF16),
+            jax.ShapeDtypeStruct((cells, CH), F32),
             jax.ShapeDtypeStruct((cells, CH), F32),
         ),
         in_specs=[hbm, smem, vmem, hbm, vmem, hbm, hbm],
@@ -654,7 +661,7 @@
         cotangent.reshape(cells, CH),
     )
     shape = (HEIGHT, WIDTH, CH)
-    return out.reshape(shape), grad.reshape(shape)
+    return out.astype(BF16).reshape(shape), grad.reshape(shape)
 
 
 def solution(mesh):

time: 105 us -> 105 us (level)
  other arithmetic: 0 us -> 1.87 us
  local copies, waits for them, and re-layouts: 2.58 us -> 0.82 us
    convert_element_type x0 -> x1, other arithmetic: none -> 1.87 us  [local(): return (out.astype(BF16).reshape(shape), grad.reshape(shape))]
    unnamed x4 -> x3, local copies, waits for them, and re-layouts: 2.58 us -> 0.82 us
where the time goes in v7:
time: 105 us
  Pallas kernels  102 us (97%)
  other arithmetic  1.87 us (2%)
    pallas_call x1, Pallas kernels, local(): pl.pallas_call(kernel, out_shape=(jax.ShapeDtypeStruct((cells, CH), F32),...  102 us

profile of v7, /device:TPU:1, one launch (start us, length us, event | category | flops | bytes accessed | tf_op | source)
XLA Modules:
  0.0 105.1 jit_solution(1662730079892635440)
XLA Ops:
  0.6 101.7 %shard_map.86 = (f32[1152,128]{1,0:T(8,128)}, f32[1152,128]{1,0:T(8,128)}) custom-call(bf16[1152,128]{1,0:T(8,128)(2,1)} %bitcast.5, s32[8]{0:T(128)} %length_ref.1, f32[2,128]{1,0:T(2,128)} %ig_ref.1, bf16[2,128,640]{2,1,0:T(8,128)(2,1)} %iw_hbm.1, f32[2,128]{1,0:T(2,128)} %og_ref.1, bf16[2,128,128]{2,1,0:T(8,128)(2,1)} %ow_hbm.1, bf16[1152,128]{1,0:T(8,128)(2,1)} %bitcast.6), custom_call_target="tpu_custom_call" | custom-call | tf_op jit(solution)/shard_map/pallas_call | solution.py:605
  102.4 0.0 copy-start
  102.4 1.9 %convert_element_type.3 = bf16[1152,128]{1,0:T(8,128)(2,1)} convert(f32[1152,128]{1,0:T(8,128)} %get-tuple-element.4) | non-fusion elementwise | flops 147456 | bytes 884736 | tf_op jit(solution)/shard_map/convert_element_type | solution.py:664
  104.3 0.0 copy-done
  104.3 0.8 copy.10
Async XLA Ops:
  102.4 1.9 %copy-start = (f32[1152,128]{1,0:T(8,128)S(1)}, f32[1152,128]{1,0:T(8,128)}, u32[]{:S(2)}) copy-start(f32[1152,128]{1,0:T(8,128)} %get-tuple-element.5) | copy-start | bytes 1769476

commit v8 on v7

--- a/solution.py
+++ b/solution.py
@@ -597,8 +597,8 @@
     hbm = pl.BlockSpec(memory_space=pltpu.HBM)
     free = pl.BlockSpec(memory_space=pl.ANY)
     smem = pl.BlockSpec(memory_space=pltpu.SMEM)
-    wide = pltpu.VMEM((DEVICES, 5, 4, 128), BF16)
-    slim = pltpu.VMEM((DEVICES, 3, 4, 128), BF16)
+    wide = pltpu.VMEM((DEVICES + 2, 5, 4, 128), BF16)
+    slim = pltpu.VMEM((DEVICES + 2, 3, 4, 128), BF16)
     plane = pltpu.VMEM((CH, LANES), F32)
     planes = pltpu.VMEM((2, CH, LANES), F32)
     line = pltpu.VMEM((2, 1, LANES), F32)

time: 105 us -> 105 us (level)
  no operation moved by 1% of the time
where the time goes in v8:
time: 105 us
  Pallas kernels  102 us (97%)
  other arithmetic  1.87 us (2%)
    pallas_call x1, Pallas kernels, local(): pl.pallas_call(kernel, out_shape=(jax.ShapeDtypeStruct((cells, CH), F32),...  102 us

profile of v8, /device:TPU:1, one launch (start us, length us, event | category | flops | bytes accessed | tf_op | source)
XLA Modules:
  0.0 105.1 jit_solution(1964257945079307866)
XLA Ops:
  0.6 101.7 %shard_map.86 = (f32[1152,128]{1,0:T(8,128)}, f32[1152,128]{1,0:T(8,128)}) custom-call(bf16[1152,128]{1,0:T(8,128)(2,1)} %bitcast.5, s32[8]{0:T(128)} %length_ref.1, f32[2,128]{1,0:T(2,128)} %ig_ref.1, bf16[2,128,640]{2,1,0:T(8,128)(2,1)} %iw_hbm.1, f32[2,128]{1,0:T(2,128)} %og_ref.1, bf16[2,128,128]{2,1,0:T(8,128)(2,1)} %ow_hbm.1, bf16[1152,128]{1,0:T(8,128)(2,1)} %bitcast.6), custom_call_target="tpu_custom_call" | custom-call | tf_op jit(solution)/shard_map/pallas_call | solution.py:605
  102.4 0.0 copy-start
  102.4 1.9 %convert_element_type.3 = bf16[1152,128]{1,0:T(8,128)(2,1)} convert(f32[1152,128]{1,0:T(8,128)} %get-tuple-element.4) | non-fusion elementwise | flops 147456 | bytes 884736 | tf_op jit(solution)/shard_map/convert_element_type | solution.py:664
  104.3 0.0 copy-done
  104.3 0.8 copy.10
Async XLA Ops:
  102.4 1.9 %copy-start = (f32[1152,128]{1,0:T(8,128)S(1)}, f32[1152,128]{1,0:T(8,128)}, u32[]{:S(2)}) copy-start(f32[1152,128]{1,0:T(8,128)} %get-tuple-element.5) | copy-start | bytes 1769476
